TPU v7x, 32 devices: a whole 2x2x4 slice. The times are simulated.
32 devices in a mesh: replica: 8 (over y, x, core), dp: 4 (over z).
Axes of the slice: x: 2, y: 2, z: 4, core: 2. Of those that a mesh axis runs over, the one named last changes fastest.
Arguments:
- block_input: bfloat16 [64, 288, 680], P(('replica', 'dp')), may hold values from -40 to 40
- time_shift: bfloat16 [64, 680], P(('replica', 'dp')), may hold values from -4 to 4
- out_grad: bfloat16 [64, 288, 680], P(('replica', 'dp')), may hold values from -6 to 6
- params: float32 [8, 680, 680], P('replica', 'dp'), may hold values from -0.21875 to 0.21875
- first_moment: float32 [8, 680, 680], P('replica', 'dp'), may hold values from -8 to 8
- second_moment: float32 [8, 680, 680], P('replica', 'dp'), may hold values from 1 to 20
- push_weight: float32 [8], P('replica'), may hold values from 0.5 to 2
- step: int32 [1], replicated, may hold values from 0 to 999
Outputs:
- grad_input: bfloat16 [64, 288, 680], P(('replica', 'dp'))
- new_params: float32 [8, 680, 680], P('replica', 'dp')
- new_first: float32 [8, 680, 680], P('replica', 'dp')
- new_second: float32 [8, 680, 680], P('replica', 'dp')
- new_weight: float32 [8], P('replica')
All inputs are finite; a program needn't handle non-finite values.
Results may differ from a plain program's by a relative error of at most 0.006.
Values may be sent and summed in bfloat16 or wider, within the bound.
No kernel may reach another device: no remote copies, remote signals or barrier semaphores. Data moves between devices by JAX's collectives and lax.ppermute only.
A program may use at most 64 MiB of HBM per device.

v0:
```python
import functools

import jax
import jax.numpy as jnp
from jax import lax
from jax.experimental import pallas as pl
from jax.experimental.pallas import tpu as pltpu
from jax.sharding import PartitionSpec as P

GSIZE = 40

NORM_EPS = 1e-05
BETA_ONE = 0.9
BETA_TWO = 0.999
LEARN_RATE = 0.002
ADAM_EPS = 1e-08

LANES = 128
ROW_STEP = 32
UNROLL = 3
TILE_ROWS = 16
VMEM_BYTES = 16 * 1024 * 1024


def padded(rows):
    return -(-rows // TILE_ROWS) * TILE_ROWS


def packed_rows(rows):
    return padded(rows + 1)


class Packing:
    def __init__(self, rows, start, stop):
        self.rows, self.start, self.stop = rows, start, stop
        self.columns = stop - start
        self.deep = packed_rows(rows)
        self.tiles, self.rest = divmod(self.columns, LANES)
        fold = LANES // self.rest if self.rest else 1
        self.fold_rows = padded(-(-self.deep // fold))
        self.folds = [
            (first, min(self.fold_rows, self.deep - first)) for first in range(0, self.deep, self.fold_rows)
        ]
        self.height = self.tiles * self.deep + (self.fold_rows if self.rest else 0)

    def write(self, ref, block):
        for tile in range(self.tiles):
            ref[tile * self.deep : (tile + 1) * self.deep, :] = block[
                :, tile * LANES : (tile + 1) * LANES
            ].astype(ref.dtype)
        if self.rest:
            left = block[:, self.tiles * LANES :]
            parts = []
            for first, count in self.folds:
                part = left[first : first + count]
                if count < self.fold_rows:
                    part = jnp.concatenate(
                        [part, jnp.zeros((self.fold_rows - count, self.rest), part.dtype)], axis=0
                    )
                parts.append(part)
            spare = LANES - self.rest * len(parts)
            if spare:
                parts.append(jnp.zeros((self.fold_rows, spare), left.dtype))
            ref[self.tiles * self.deep :, :] = jnp.concatenate(parts, axis=1).astype(ref.dtype)

    def read(self, ref):
        pieces = [
            ref[tile * self.deep : (tile + 1) * self.deep, :].astype(jnp.float32) for tile in range(self.tiles)
        ]
        if self.rest:
            left = ref[self.tiles * self.deep :, :].astype(jnp.float32)
            parts = [
                left[:count, i * self.rest : (i + 1) * self.rest] for i, (_, count) in enumerate(self.folds)
            ]
            pieces.append(jnp.concatenate(parts, axis=0) if len(parts) > 1 else parts[0])
        return jnp.concatenate(pieces, axis=1) if len(pieces) > 1 else pieces[0]

    def unpack(self, ref, out_ref, first_row):
        for tile in range(self.tiles):
            out_ref[first_row : first_row + self.deep, tile * LANES : (tile + 1) * LANES] = ref[
                tile * self.deep : (tile + 1) * self.deep, :
            ]
        if self.rest:
            left = ref[self.tiles * self.deep :, :]
            for i, (first, count) in enumerate(self.folds):
                out_ref[first_row + first : first_row + first + count, self.tiles * LANES :] = left[
                    :count, i * self.rest : (i + 1) * self.rest
                ]

    def payload(self):
        return jax.ShapeDtypeStruct((self.height, LANES), jnp.bfloat16)

    def block(self):
        return jax.ShapeDtypeStruct((self.deep, self.columns), jnp.float32)


def group_sums(rows, same_group):
    high = rows.astype(jnp.bfloat16).astype(jnp.float32)
    rest = rows - high
    middle = rest.astype(jnp.bfloat16).astype(jnp.float32)
    count = rows.shape[0]
    stacked = jnp.concatenate([high, middle, rest - middle], axis=0).astype(jnp.bfloat16)
    sums = jnp.dot(stacked, same_group, preferred_element_type=jnp.float32)
    return sums[:count] + (sums[count : 2 * count] + sums[2 * count :])


def table_sums(packs, rows, same_group):
    return jnp.concatenate(
        [
            group_sums(rows[:, pack.start : pack.stop], same_group[: pack.columns, : pack.columns])
            for pack in packs
        ],
        axis=1,
    )


def position_sums(parts):
    return jnp.concatenate([jnp.sum(part, axis=0, keepdims=True) for part in parts], axis=0)


def doubled_silu_grad(half, turned):
    return (1.0 + turned) + half * (1.0 - turned * turned)


def row(vector, i):
    return vector[i : i + 1]


def eight_sums(block):
    return sum(block[first : first + 8] for first in range(0, block.shape[0], 8))


def squares_sums(samples, positions, step, load, offset):
    sums = []
    for i in range(samples):

        def body(k, total):
            value = load(i, pl.multiple_of(k * step, step), step) + row(offset, i)
            return total + eight_sums(value * value)

        total = lax.fori_loop(0, positions // step, body, jnp.zeros((8, offset.shape[1]), jnp.float32), unroll=UNROLL)
        sums.append(jnp.sum(total, axis=0, keepdims=True))
    return jnp.concatenate(sums, axis=0)


def norm_back(table_mean, samples, positions, step, load, scales, offsets, inverse, incoming, kept_ref, store):
    firsts, seconds = [], []
    zeros = jnp.zeros((8, scales.shape[1]), jnp.float32)
    for i in range(samples):

        def body(k, totals):
            first_row = pl.multiple_of(k * step, step)
            half = load(i, first_row, step) * row(scales, i) + row(offsets, i)
            doubled = incoming(i, first_row, step) * doubled_silu_grad(half, jnp.tanh(half))
            kept_ref[pl.ds(pl.multiple_of(i * positions + first_row, step), step), :] = doubled
            return totals[0] + eight_sums(doubled), totals[1] + eight_sums(doubled * half)

        first, second = lax.fori_loop(0, positions // step, body, (zeros, zeros), unroll=UNROLL)
        firsts.append(jnp.sum(first, axis=0, keepdims=True))
        seconds.append(jnp.sum(second, axis=0, keepdims=True))
    means = table_mean(jnp.concatenate(firsts + seconds, axis=0))
    first, second = 0.5 * means[:samples], means[samples:]
    gain = 0.5 * inverse
    slope = (2.0 * inverse) * second * scales
    level = inverse * (first + 2.0 * offsets * second)
    for i in range(samples):

        def body(k, carry):
            first_row = pl.multiple_of(k * step, step)
            doubled = kept_ref[pl.ds(pl.multiple_of(i * positions + first_row, step), step), :]
            value = load(i, first_row, step)
            store(i, first_row, step, doubled * row(gain, i) - (value * row(slope, i) + row(level, i)))
            return carry

        lax.fori_loop(0, positions // step, body, 0, unroll=UNROLL)


def sigmoid(values):
    return 0.5 * jnp.tanh(0.5 * values) + 0.5


def silu_grad(values):
    gate = sigmoid(values)
    return gate * (1.0 + values * (1.0 - gate))


def cast_kernel(pack, push_ref, params_ref, token_ref, other_token_ref, out_ref, rows_ref):
    rows = pack.rows
    rows_ref[rows // 8 * 8 :, :] = jnp.zeros((pack.deep - rows // 8 * 8, pack.columns), jnp.float32)
    rows_ref[:rows, :] = params_ref[:, 0, pack.start : pack.stop] / push_ref[...]
    pack.write(out_ref, rows_ref[...])


def norm_in_kernel(shards, packs, me_ref, scales_ref, shift_ref, x_hbm, out_grad_hbm, *refs):
    act_ref, mean_ref, inverse_ref, same_group_ref = refs[:4]
    shift_refs, out_grad_refs = refs[4 : 4 + len(packs)], refs[4 + len(packs) : 4 + 2 * len(packs)]
    x_ref, out_grad_ref, sems = refs[4 + 2 * len(packs) :]
    copies = [
        pltpu.make_async_copy(x_hbm, x_ref, sems.at[0]),
        pltpu.make_async_copy(out_grad_hbm, out_grad_ref, sems.at[1]),
    ]
    for copy in copies:
        copy.start()
    samples, positions, channels = x_ref.shape
    rows = channels // shards
    deep = act_ref.shape[0] // shards
    entries = positions * GSIZE
    group_of_row = lax.broadcasted_iota(jnp.int32, same_group_ref.shape, 0) // GSIZE
    group_of_column = lax.broadcasted_iota(jnp.int32, same_group_ref.shape, 1) // GSIZE
    same_group_ref[...] = (group_of_row == group_of_column).astype(jnp.float32).astype(jnp.bfloat16)
    same_group = same_group_ref[...]
    for pack, shift_out in zip(packs, shift_refs):
        shift_out[...] = shift_ref[...].astype(jnp.float32)[:, pack.start : pack.stop]
    copies[0].wait()
    parts = [x_ref[i].astype(jnp.float32) for i in range(samples)]
    mean = table_sums(packs, position_sums(parts), same_group) / entries
    centered = [parts[i] - mean[i : i + 1] for i in range(samples)]
    variance = table_sums(packs, position_sums([part * part for part in centered]), same_group) / entries
    inverse = lax.rsqrt(variance + NORM_EPS)
    mean_ref[...] = mean
    inverse_ref[...] = inverse
    normed = [centered[i] * inverse[i : i + 1] for i in range(samples)]
    act = jnp.concatenate([part * sigmoid(part) for part in normed], axis=0).T
    for block in range(shards):
        slot = jnp.bitwise_xor(me_ref[0], block)
        act_ref[pl.ds(pl.multiple_of(slot * deep, TILE_ROWS), deep), :] = jnp.concatenate(
            [act[block * rows : (block + 1) * rows], jnp.zeros((deep - rows, act.shape[1]), jnp.float32)], axis=0
        ).astype(jnp.bfloat16)
    copies[1].wait()
    for pack, out_grad_out in zip(packs, out_grad_refs):
        for i in range(samples):
            out_grad_out[i] = out_grad_ref[i][:, pack.start : pack.stop]


def mix_kernel(shards, pack, act_ref, shift_ref, out_grad_ref, same_group_ref, *refs):
    weight_refs, token_ref, refs = refs[:shards], refs[shards], refs[shards + 1 :]
    grad_hidden_ref, weight_out_ref, own_ref = refs[:3]
    send_refs, (weight_ref, kept_ref, hidden_ref, doubled_ref, sems) = refs[3 : 2 + shards], refs[2 + shards :]
    samples, positions, columns = out_grad_ref.shape
    entries = positions * GSIZE
    deep = pack.deep
    for slot, shard_ref in enumerate(weight_refs):
        pack.unpack(shard_ref, weight_ref, slot * deep)
    weight_copy = pltpu.make_async_copy(weight_ref, weight_out_ref, sems.at[0])
    weight_copy.start()
    same_group = same_group_ref[:columns, :columns]
    hidden_ref[...] = lax.dot_general(
        act_ref[...], weight_ref[...], (((0,), (0,)), ((), ())), preferred_element_type=jnp.float32
    )

    def table_mean(rows):
        return group_sums(rows, same_group) / entries

    def load(i, first_row, count):
        return hidden_ref[pl.ds(pl.multiple_of(i * positions + first_row, count), count), :]

    def incoming(i, first_row, count):
        return out_grad_ref[i, pl.ds(first_row, count), :].astype(jnp.float32)

    def store(i, first_row, count, grad):
        kept_ref[pl.ds(pl.multiple_of(i * positions + first_row, count), count), :] = grad.astype(jnp.bfloat16)

    shift = shift_ref[...]
    sums = position_sums([hidden_ref[i * positions : (i + 1) * positions, :] for i in range(samples)])
    offset = shift - table_mean(sums + positions * shift)
    squares = squares_sums(samples, positions, ROW_STEP, load, offset)
    inverse = lax.rsqrt(table_mean(squares) + NORM_EPS)
    scales = 0.5 * inverse
    norm_back(
        table_mean, samples, positions, ROW_STEP, load, scales, offset * scales, inverse, incoming, doubled_ref, store
    )
    copy = pltpu.make_async_copy(kept_ref, grad_hidden_ref, sems.at[1])
    copy.start()
    grad = jnp.dot(act_ref[...], kept_ref[...], preferred_element_type=jnp.float32)
    for slot, send_ref in enumerate(send_refs, 1):
        pack.write(send_ref, grad[slot * deep : (slot + 1) * deep])
    own_ref[...] = grad[:deep]
    weight_copy.wait()
    copy.wait()


def input_grad_kernel(shards, packs, me_ref, mean_ref, inverse_ref, same_group_ref, x_hbm, *refs):
    count = len(packs)
    grad_refs, weight_refs, out_ref = refs[:count], refs[count : 2 * count], refs[2 * count]
    rows_ref, x_ref, made_ref, act_ref, sems = refs[2 * count + 1 :]
    copies = [pltpu.make_async_copy(x_hbm, x_ref, sems.at[0])]
    copies[0].start()
    samples, positions, channels = x_ref.shape
    entries = positions * GSIZE
    rows = channels // shards
    weights = []
    for index, (pack, weight_ref) in enumerate(zip(packs, weight_refs)):
        for block in range(shards):
            slot = jnp.bitwise_xor(me_ref[0], block)
            rows_ref[block * rows : (block + 1) * rows, : pack.columns] = weight_ref[
                pl.ds(pl.multiple_of(slot * pack.deep, TILE_ROWS), pack.deep), :
            ].astype(jnp.float32)[:rows]
        weights.append(rows_ref[:, : pack.columns].astype(jnp.bfloat16))
    grad_act = 0.0
    for index, (grad_ref, weight) in enumerate(zip(grad_refs, weights)):
        grad_act += lax.dot_general(
            grad_ref[...], weight, (((1,), (1,)), ((), ())), preferred_element_type=jnp.float32
        )
    act_ref[...] = grad_act
    copies[0].wait()
    same_group = same_group_ref[...]
    inverse = inverse_ref[...]

    def table_mean(rows):
        return table_sums(packs, rows, same_group) / entries

    def load(i, first_row, count):
        return x_ref[i, pl.ds(first_row, count), :].astype(jnp.float32)

    def incoming(i, first_row, count):
        return act_ref[pl.ds(pl.multiple_of(i * positions + first_row, count), count), :]

    def store(i, first_row, count, grad):
        made_ref[i, pl.ds(first_row, count), :] = grad.astype(jnp.bfloat16)

    scales = 0.5 * inverse
    norm_back(
        table_mean, samples, positions, ROW_STEP, load, scales, -mean_ref[...] * scales, inverse, incoming, act_ref, store
    )
    for i in range(samples):
        copies.append(pltpu.make_async_copy(made_ref.at[i], out_ref.at[i], sems.at[len(copies)]))
        copies[-1].start()
    for copy in copies[-samples:]:
        copy.wait()


def merge_kernel(one_ref, other_ref, *refs):
    count = len(refs) // 2
    through_refs, out_ref, through_out_refs = refs[:count], refs[count], refs[count + 1 :]
    out_ref[...] = (one_ref[...].astype(jnp.float32) + other_ref[...].astype(jnp.float32)).astype(out_ref.dtype)
    for through_ref, through_out_ref in zip(through_refs, through_out_refs):
        through_out_ref[...] = through_ref[...]


def cut_kernel(packs, *refs):
    count = 3 * len(packs)
    hbm_refs, out_refs = refs[:3], refs[4 : 4 + count]
    row_refs, block_refs, sems = refs[4 + count : 7 + count], refs[7 + count : -1], refs[-1]
    copies = [
        pltpu.make_async_copy(source, target, sems.at[i])
        for i, (source, target) in enumerate(zip(hbm_refs, row_refs))
    ]
    for copy in copies:
        copy.start()
    out_copies = []
    for i, row_ref in enumerate(row_refs):
        copies[i].wait()
        for index, pack in enumerate(packs):
            place = 3 * index + i
            block_refs[place][...] = row_ref[:, 0, pack.start : pack.stop]
            out_copies.append(pltpu.make_async_copy(block_refs[place], out_refs[place], sems.at[3 + place]))
            out_copies[-1].start()
    for copy in out_copies:
        copy.wait()


def adam_kernel(count, pack, spare_value, scales_ref, own_ref, *refs):
    other_refs, refs = refs[:count], refs[count:]
    (params_ref, first_ref, second_ref), (grad_ref, moved_ref, sent_ref) = refs[:3], refs[-3:]
    rows = pack.rows
    total = own_ref[...]
    for other_ref in other_refs:
        total = total + pack.read(other_ref)
    grad_ref[...] = total * scales_ref[2]
    grad = grad_ref[:rows, :]
    first_new = BETA_ONE * first_ref[...] + (1.0 - BETA_ONE) * grad
    second_new = BETA_TWO * second_ref[...] + (1.0 - BETA_TWO) * grad * grad
    update = (scales_ref[0] * first_new) / (jnp.sqrt(second_new * scales_ref[1]) + ADAM_EPS)
    value = scales_ref[3] if spare_value else 0.0
    moved_ref[rows // 8 * 8 :, :] = jnp.full((pack.deep - rows // 8 * 8, pack.columns), value, jnp.float32)
    moved_ref[:rows, :] = params_ref[...] - update
    pack.write(sent_ref, moved_ref[...])


def half_average_kernel(pack, scales_ref, moved_ref, other_ref, mean_ref, push_out_ref):
    other = pack.read(other_ref)
    mean_ref[...] = 0.5 * (moved_ref[...] + other)
    push_out_ref[...] = 0.5 * (scales_ref[3] + other[pack.rows, :1])


def moments_kernel(packs, first_hbm, second_hbm, *refs):
    grad_refs, (first_out, second_out, first_ref, second_ref, sems) = refs[: len(packs)], refs[len(packs) :]
    copies = [
        pltpu.make_async_copy(first_hbm, first_ref, sems.at[0]),
        pltpu.make_async_copy(second_hbm, second_ref, sems.at[1]),
    ]
    for copy in copies:
        copy.start()
    rows = first_ref.shape[0]
    grad = jnp.concatenate([grad_ref[:rows, :] for grad_ref in grad_refs], axis=1)
    copies[0].wait()
    first_out[:, 0, :] = BETA_ONE * first_ref[:, 0, :] + (1.0 - BETA_ONE) * grad
    copies[1].wait()
    second_out[:, 0, :] = BETA_TWO * second_ref[:, 0, :] + (1.0 - BETA_TWO) * grad * grad


def average_kernel(pack, mean_ref, moved_ref, other_ref, out_ref, rows_ref, sem):
    rows = out_ref.shape[0]
    later = 0.5 * (moved_ref[...] + pack.read(other_ref))
    rows_ref[:, 0, :] = jnp.concatenate([mean_ref[...], later], axis=1)[:rows]
    copy = pltpu.make_async_copy(rows_ref, out_ref, sem)
    copy.start()
    copy.wait()


SCALARS = pl.BlockSpec(memory_space=pltpu.SMEM)
BLOCKS = pl.BlockSpec(memory_space=pltpu.VMEM)
TOKEN = pl.BlockSpec(memory_space=pl.ANY)
IN_HBM = pl.BlockSpec(memory_space=pltpu.HBM)


def call(kernel, name, outs, specs, operands, scratch=(), out_specs=None, flops=0, elements=0):
    return pl.pallas_call(
        kernel,
        out_shape=outs,
        in_specs=specs,
        out_specs=out_specs or jax.tree.map(lambda _: BLOCKS, outs),
        scratch_shapes=list(scratch),
        compiler_params=pltpu.CompilerParams(vmem_limit_bytes=VMEM_BYTES),
        cost_estimate=pl.CostEstimate(flops=flops, bytes_accessed=8 * elements, transcendentals=elements),
        name=name,
    )(*operands)


def stay(array):
    return pltpu.with_memory_space_constraint(array, pltpu.HBM)


def moved_on(block, axis, distance):
    size = lax.axis_size(axis)
    return lax.ppermute(block, axis, [(i, (i + distance) % size) for i in range(size)])


def exchanged(block, axis, bit):
    return lax.ppermute(block, axis, [(i, i ^ bit) for i in range(lax.axis_size(axis))])


def lowest_bit(slot):
    return slot & -slot


def hold_kernel(block_ref, token_ref, out_ref):
    out_ref[...] = block_ref[...]


def gathered(piece, shards, token=None):
    held = [piece]
    for slot in range(1, shards):
        bit = lowest_bit(slot)
        held.append(exchanged(held[slot ^ bit], "dp", bit))
        if token is not None and slot == 2:
            shape = jax.ShapeDtypeStruct(piece.shape, piece.dtype)
            held[slot] = call(hold_kernel, "hold", shape, [BLOCKS, IN_HBM], (held[slot], stay(token)))
    return held


def scattered(parts, shards):
    arrived = []
    for part, sends in enumerate(parts):
        held = dict(enumerate(sends, 1))
        slots = sorted(range(2, shards), key=lambda slot: (-slot.bit_count(), -slot))
        last = part == len(parts) - 1
        got = [] if last else [exchanged(held[1], "dp", 1)]
        for slot in slots:
            bit = lowest_bit(slot)
            other = exchanged(held[slot], "dp", bit)
            if slot == bit:
                got.append(other)
                continue
            shape = jax.ShapeDtypeStruct(other.shape, other.dtype)
            held[slot ^ bit], held[1] = call(
                merge_kernel, "merge", (shape,) * 2, [BLOCKS] * 3, (held[slot ^ bit], other, held[1] if last else got[0])
            )
        if last:
            got.append(exchanged(held[1], "dp", 1))
        else:
            got[0] = held[1]
        arrived.append(got)
    return arrived


def column_cuts(channels):
    half = (channels // GSIZE + 1) // 2 * GSIZE
    return [(0, half), (half, channels)]


def local(
    block_input, time_shift, out_grad, params, first_moment, second_moment, push_weight, step
):
    samples, positions, channels = block_input.shape
    tokens = samples * positions
    shards = lax.axis_size("dp")
    rows = params.shape[1]
    deep = packed_rows(rows)
    me = lax.axis_index("dp").astype(jnp.int32).reshape(1)
    packs = [Packing(rows, start, stop) for start, stop in column_cuts(channels)]
    params, first_moment, second_moment = (
        jnp.transpose(array, (1, 0, 2)) for array in (params, first_moment, second_moment)
    )
    def shards_of(pack, *tokens, late=None):
        piece = call(
            functools.partial(cast_kernel, pack),
            "cast",
            pack.payload(),
            [BLOCKS, BLOCKS, TOKEN, TOKEN],
            (push_weight.reshape(1, 1), params, *tokens),
            scratch=[pltpu.VMEM((deep, pack.columns), jnp.float32)],
            elements=rows * pack.columns,
        )
        return gathered(piece, shards, late)

    level_count = lax.axis_size("replica").bit_length() - 1
    distance_bits = step[0] % level_count
    step_count = (step[0] + 1).astype(jnp.float32)
    scales = jnp.stack(
        [
            LEARN_RATE / (1.0 - jnp.power(BETA_ONE, step_count)),
            1.0 / (1.0 - jnp.power(BETA_TWO, step_count)),
            jnp.float32(1.0 / shards),
            push_weight[0],
        ]
    )

    activation, mean_in, inverse_in, same_group, *pieces = call(
        functools.partial(norm_in_kernel, shards, packs),
        "norm_in",
        (
            jax.ShapeDtypeStruct((shards * deep, tokens), jnp.bfloat16),
            jax.ShapeDtypeStruct((samples, channels), jnp.float32),
            jax.ShapeDtypeStruct((samples, channels), jnp.float32),
            jax.ShapeDtypeStruct((max(pack.columns for pack in packs),) * 2, jnp.bfloat16),
            *(jax.ShapeDtypeStruct((samples, pack.columns), jnp.float32) for pack in packs),
            *(jax.ShapeDtypeStruct((samples, positions, pack.columns), jnp.bfloat16) for pack in packs),
        ),
        [SCALARS, SCALARS, BLOCKS, IN_HBM, IN_HBM],
        (me, scales, time_shift, stay(block_input), stay(out_grad)),
        scratch=[
            pltpu.VMEM(block_input.shape, jnp.bfloat16),
            pltpu.VMEM(out_grad.shape, jnp.bfloat16),
            pltpu.SemaphoreType.DMA((2,)),
        ],
        elements=tokens * channels,
    )

    columns = [pack.columns for pack in packs for _ in range(3)]
    blocks = call(
        functools.partial(cut_kernel, packs),
        "cut",
        tuple(pltpu.HBM((rows, width), jnp.float32) for width in columns),
        [IN_HBM] * 3 + [TOKEN],
        (stay(params), stay(first_moment), stay(second_moment), mean_in),
        scratch=[pltpu.VMEM(params.shape, jnp.float32)] * 3
        + [pltpu.VMEM((rows, width), jnp.float32) for width in columns]
        + [pltpu.SemaphoreType.DMA((3 + len(columns),))],
        out_specs=(IN_HBM,) * len(columns),
        elements=rows * channels,
    )
    weights = [shards_of(packs[0], params, params)]
    weights.append(shards_of(packs[1], weights[0][1], mean_in, late=blocks[-1]))
    hidden_grads, full_weights, owns, parts = [], [], [], []
    token = mean_in
    shifts, out_grads = pieces[: len(packs)], pieces[len(packs) :]
    for pack, shard_list, shift, out_grad_piece in zip(packs, weights, shifts, out_grads):
        kept = jax.ShapeDtypeStruct if pack is packs[-1] else pltpu.HBM
        kept_spec = BLOCKS if pack is packs[-1] else IN_HBM
        grad_hidden, full_weight, own, *sends = call(
            functools.partial(mix_kernel, shards, pack),
            "mix",
            (
                kept((tokens, pack.columns), jnp.bfloat16),
                kept((shards * deep, pack.columns), jnp.bfloat16),
                pack.block(),
            )
            + (pack.payload(),) * (shards - 1),
            [BLOCKS] * (4 + shards) + [TOKEN],
            (activation, shift, out_grad_piece, same_group, *shard_list, token),
            scratch=[
                pltpu.VMEM((shards * deep, pack.columns), jnp.bfloat16),
                pltpu.VMEM((tokens, pack.columns), jnp.bfloat16),
                pltpu.VMEM((tokens, pack.columns), jnp.float32),
                pltpu.VMEM((tokens, pack.columns), jnp.float32),
                pltpu.SemaphoreType.DMA((2,)),
            ],
            out_specs=(kept_spec,) * 2 + (BLOCKS,) * shards,
            flops=4 * tokens * channels * pack.columns,
            elements=tokens * pack.columns,
        )
        token = own
        hidden_grads.append(grad_hidden)
        full_weights.append(full_weight)
        owns.append(own)
        parts.append(sends)

    def input_grad(*operands):
        return call(
            functools.partial(input_grad_kernel, shards, packs),
            "input_grad",
            pltpu.HBM(block_input.shape, jnp.bfloat16),
            [SCALARS] + [BLOCKS] * 3 + [IN_HBM] + [BLOCKS] * (2 * len(packs)),
            operands[:4] + (stay(operands[4]),) + operands[5:],
            scratch=[
                pltpu.VMEM((channels, max(pack.columns for pack in packs)), jnp.float32),
                pltpu.VMEM(block_input.shape, jnp.bfloat16),
                pltpu.VMEM(block_input.shape, jnp.bfloat16),
                pltpu.VMEM((tokens, channels), jnp.float32),
                pltpu.SemaphoreType.DMA((1 + samples,)),
            ],
            out_specs=IN_HBM,
            flops=2 * tokens * channels * channels,
            elements=tokens * channels,
        )

    def moments(*grads):
        return call(
            functools.partial(moments_kernel, packs),
            "moments",
            (jax.ShapeDtypeStruct(params.shape, jnp.float32),) * 2,
            [IN_HBM] * 2 + [BLOCKS] * len(packs),
            (stay(first_moment), stay(second_moment), *grads),
            scratch=[pltpu.VMEM(params.shape, jnp.float32)] * 2 + [pltpu.SemaphoreType.DMA((2,))],
            elements=rows * channels,
        )

    def from_behind(finish, *operands):
        def branch(distance):
            return lambda *values: finish(lambda block: moved_on(block, "replica", distance), *values)

        return lax.switch(distance_bits, [branch(1 << power) for power in range(level_count)], *operands)

    grad_input = input_grad(
        me, mean_in, inverse_in, same_group, block_input, *hidden_grads, *full_weights
    )
    arrived = scattered(parts, shards)
    early, late = packs

    def adam(pack, own, others, blocks):
        return call(
            functools.partial(adam_kernel, len(others), pack, pack is early),
            "adam",
            (pack.block(), pack.block(), pack.payload()),
            [SCALARS] + [BLOCKS] * (4 + len(others)),
            (scales, own, *others, *blocks),
            elements=rows * pack.columns,
        )

    grad_a, moved_a, sent_a = adam(early, owns[0], arrived[0], blocks[:3])

    def finish(move, sent, grad_a, moved_a, own, *operands):
        other_a = move(sent)
        grad_b, moved_b, sent_b = adam(late, own, operands[:-3], operands[-3:])
        other_b = move(sent_b)
        mean, weight = call(
            functools.partial(half_average_kernel, early),
            "half_average",
            (early.block(), jax.ShapeDtypeStruct((1,), jnp.float32)),
            [SCALARS] + [BLOCKS] * 2,
            (scales, moved_a, other_a),
            elements=rows * early.columns,
        )
        averaged = call(
            functools.partial(average_kernel, late),
            "average",
            pltpu.HBM(params.shape, jnp.float32),
            [BLOCKS] * 3,
            (mean, moved_b, other_b),
            scratch=[pltpu.VMEM(params.shape, jnp.float32), pltpu.SemaphoreType.DMA],
            out_specs=IN_HBM,
            elements=rows * channels,
        )
        return (*moments(grad_a, grad_b), averaged, weight)

    first_new, second_new, averaged, new_weight = from_behind(
        finish, sent_a, grad_a, moved_a, owns[1], *arrived[1], *blocks[3:]
    )
    return (
        grad_input,
        *(jnp.transpose(array, (1, 0, 2)) for array in (averaged, first_new, second_new)),
        new_weight,
    )


def solution(mesh):
    placed = (
        P(("replica", "dp"), None, None),
        P(("replica", "dp"), None),
        P(("replica", "dp"), None, None),
        P("replica", "dp", None),
        P("replica", "dp", None),
        P("replica", "dp", None),
        P("replica"),
        P(),
    )
    return jax.shard_map(
        local,
        mesh=mesh,
        in_specs=placed,
        out_specs=(
            P(("replica", "dp"), None, None),
            P("replica", "dp", None),
            P("replica", "dp", None),
            P("replica", "dp", None),
            P("replica"),
        ),
        check_vma=False,
    )
```

profile of v0, /device:TPU:0, one launch (start us, length us, event | category | flops | bytes accessed | tf_op | source)
XLA Modules:
  0.0 53.7 jit_solution(16751217872209678552)
XLA Ops:
  1.3 0.0 copy-start
  1.3 1.0 %copy-done = f32[1,170,680]{2,0,1:T(1,128)S(1)} copy-done((f32[1,170,680]{2,0,1:T(1,128)S(1)}, f32[1,170,680]{2,0,1:T(1,128)}, u32[]{:S(2)}) %copy-start) | copy-done | bytes 462424
  2.3 0.2 cast.2.refs_0_
  2.5 3.1 %collective-permute-start.6 = (bf16[528,128]{1,0:T(8,128)(2,1)S(1)}, bf16[528,128]{1,0:T(8,128)(2,1)S(1)}, u32[]{:S(2)}, u32[]{:S(2)}) collective-permute-start(bf16[528,128]{1,0:T(8,128)(2,1)S(1)} %cast.2.refs_0_), channel_id=1, source_target_pairs={{0,1},{1,0},{2,3},{3,2},{4,5},{5,4},{6,7},{7,6},{8,9},{9,8},{10,11... | collective-permute-start | bytes 405512 | tf_op jit(solution)/shard_map/ppermute | solution.py:440
  5.6 2.6 %collective-permute-start.7 = (bf16[528,128]{1,0:T(8,128)(2,1)S(1)}, bf16[528,128]{1,0:T(8,128)(2,1)S(1)}, u32[]{:S(2)}, u32[]{:S(2)}) collective-permute-start(bf16[528,128]{1,0:T(8,128)(2,1)S(1)} %cast.2.refs_0_), channel_id=1, source_target_pairs={{0,2},{1,3},{2,0},{3,1},{4,6},{5,7},{6,4},{7,5},{8,10},{9,11},{10,... | collective-permute-start | bytes 405512 | tf_op jit(solution)/shard_map/ppermute | solution.py:440
  9.0 0.0 copy-start.7
  9.0 0.1 pad_maximum_fusion.scales_ref
  9.1 0.6 %copy-done.7 = bf16[2,680]{1,0:T(2,128)(2,1)S(1)} copy-done((bf16[2,680]{1,0:T(2,128)(2,1)S(1)}, bf16[2,680]{1,0:T(2,128)(2,1)}, u32[]{:S(2)}) %copy-start.7) | copy-done | bytes 2744
  9.7 3.4 %norm_in.1 = (bf16[704,576]{1,0:T(8,128)(2,1)S(1)}, f32[2,680]{1,0:T(2,128)S(1)}, f32[2,680]{1,0:T(2,128)S(1)}, bf16[360,360]{1,0:T(8,128)(2,1)S(1)}, f32[2,360]...) custom-call(s32[1]{0:T(128)} %bitcast.3.me_ref, ...), custom_call_target="tpu_custom_call" | custom-call | bytes 3133440 | tf_op jit(solution)/shard_map/norm_in/pallas_call | solution.py:418
  13.0 0.0 collective-permute-done.6.refs_1_.token_ref
  13.0 0.0 copy-done.1
  13.0 0.3 cast.3.refs_0_
  13.3 0.4 collective-permute-start.10
  13.7 0.8 %collective-permute-done.7.refs_2_ = bf16[528,128]{1,0:T(8,128)(2,1)S(1)} collective-permute-done((bf16[528,128]{1,0:T(8,128)(2,1)S(1)}, bf16[528,128]{1,0:T(8,128)(2,1)S(1)}, u32[]{:S(2)}, u32[]{:S(2)}) %collective-permute-start.7) | collective-permute-done | bytes 135200 | tf_op jit(solution)/shard_map/ppermute | solution.py:440
  14.5 1.0 %collective-permute-start.8 = (bf16[528,128]{1,0:T(8,128)(2,1)S(1)}, bf16[528,128]{1,0:T(8,128)(2,1)S(1)}, u32[]{:S(2)}, u32[]{:S(2)}) collective-permute-start(bf16[528,128]{1,0:T(8,128)(2,1)S(1)} %collective-permute-done.7.refs_2_), channel_id=1, source_target_pairs={{0,1},{1,0},{2,3},{3,2},{4,5},{5,4},{6,7},{7,6},{8,9},{9,8},{10,11... | collective-permute-start | bytes 405512 | tf_op jit(solution)/shard_map/ppermute | solution.py:440
  15.5 2.4 %cut.1 = (f32[170,360]{1,0:T(8,128)}, f32[170,360]{1,0:T(8,128)}, f32[170,360]{1,0:T(8,128)}, f32[170,320]{1,0:T(8,128)}, f32[170,320]{1,0:T(8,128)}, /*index=5*/f32[170,320]{1,0:T(8,128)}) custom-call(f32[170,1,680]{2,1,0:T(1,128)} %bitcast.13, f32[170,1,680]{2,1,0:T(1,128)} %bitcast.18, f32[170,1,680]{2,1,0:T(1,128)} %bitcast.22, ...), custom_call_target="tpu_custom_call" | custom-call | bytes 924800 | tf_op jit(solution)/shard_map/cut/pallas_call | solution.py:418
  18.0 1.0 %collective-permute-start.9 = (bf16[448,128]{1,0:T(8,128)(2,1)S(1)}, bf16[448,128]{1,0:T(8,128)(2,1)S(1)}, u32[]{:S(2)}, u32[]{:S(2)}) collective-permute-start(bf16[448,128]{1,0:T(8,128)(2,1)S(1)} %cast.3.refs_0_), channel_id=1, source_target_pairs={{0,1},{1,0},{2,3},{3,2},{4,5},{5,4},{6,7},{7,6},{8,9},{9,8},{10,11... | collective-permute-start | bytes 344072 | tf_op jit(solution)/shard_map/ppermute | solution.py:440
  19.0 2.1 %collective-permute-done.10.block_ref = bf16[448,128]{1,0:T(8,128)(2,1)S(1)} collective-permute-done((bf16[448,128]{1,0:T(8,128)(2,1)S(1)}, bf16[448,128]{1,0:T(8,128)(2,1)S(1)}, u32[]{:S(2)}, u32[]{:S(2)}) %collective-permute-start.10) | collective-permute-done | bytes 114720 | tf_op jit(solution)/shard_map/ppermute | solution.py:440
  21.1 0.1 collective-permute-start.11
  21.2 1.2 %collective-permute-done.8.refs_3_ = bf16[528,128]{1,0:T(8,128)(2,1)S(1)} collective-permute-done((bf16[528,128]{1,0:T(8,128)(2,1)S(1)}, bf16[528,128]{1,0:T(8,128)(2,1)S(1)}, u32[]{:S(2)}, u32[]{:S(2)}) %collective-permute-start.8) | collective-permute-done | bytes 135200 | tf_op jit(solution)/shard_map/ppermute | solution.py:440
  22.3 2.7 %mix.2 = (bf16[576,360]{1,0:T(8,128)(2,1)}, bf16[704,360]{1,0:T(8,128)(2,1)}, f32[176,360]{1,0:T(8,128)S(1)}, bf16[528,128]{1,0:T(8,128)(2,1)S(1)}, bf16[528,128...) custom-call(bf16[704,576]{1,0:T(8,128)(2,1)S(1)} %get-tuple-element.175.act_ref, ...), custom_call_target="tpu_custom_call" | custom-call | flops 564019200 | bytes 1658880 | tf_op jit(solution)/shard_map/mix/pallas_call | solution.py:418
  25.1 0.9 %collective-permute-start.15 = (bf16[528,128]{1,0:T(8,128)(2,1)S(1)}, bf16[528,128]{1,0:T(8,128)(2,1)S(1)}, u32[]{:S(2)}, u32[]{:S(2)}) collective-permute-start(bf16[528,128]{1,0:T(8,128)(2,1)S(1)} %get-tuple-element.195), channel_id=1, source_target_pairs={{0,1},{1,0},{2,3},{3,2},{4,5},{5,4},{6,7},{7,6},{8,9},{9,8},{10,11... | collective-permute-start | bytes 405512 | tf_op jit(solution)/shard_map/ppermute | solution.py:440
  26.0 1.2 %collective-permute-start.16 = (bf16[528,128]{1,0:T(8,128)(2,1)S(1)}, bf16[528,128]{1,0:T(8,128)(2,1)S(1)}, u32[]{:S(2)}, u32[]{:S(2)}) collective-permute-start(bf16[528,128]{1,0:T(8,128)(2,1)S(1)} %get-tuple-element.196), channel_id=1, source_target_pairs={{0,1},{1,0},{2,3},{3,2},{4,5},{5,4},{6,7},{7,6},{8,9},{9,8},{10,11... | collective-permute-start | bytes 405512 | tf_op jit(solution)/shard_map/ppermute | solution.py:440
  27.2 0.0 collective-permute-done.9.refs_1_
  27.2 0.0 collective-permute-done.11.refs_3_
  27.2 3.2 %mix.3 = (bf16[576,320]{1,0:T(8,128)(2,1)S(1)}, bf16[704,320]{1,0:T(8,128)(2,1)S(1)}, f32[176,320]{1,0:T(8,128)S(1)}, bf16[448,128]{1,0:T(8,128)(2,1)S(1)}, bf16...) custom-call(bf16[704,576]{1,0:T(8,128)(2,1)S(1)} %get-tuple-element.175.act_ref, ...), custom_call_target="tpu_custom_call" | custom-call | flops 501350400 | bytes 1474560 | tf_op jit(solution)/shard_map/mix/pallas_call | solution.py:418
  30.4 0.0 copy-start.2
  30.4 0.9 %collective-permute-start.12 = (bf16[448,128]{1,0:T(8,128)(2,1)S(1)}, bf16[448,128]{1,0:T(8,128)(2,1)S(1)}, u32[]{:S(2)}, u32[]{:S(2)}) collective-permute-start(bf16[448,128]{1,0:T(8,128)(2,1)S(1)} %get-tuple-element.188), channel_id=1, source_target_pairs={{0,1},{1,0},{2,3},{3,2},{4,5},{5,4},{6,7},{7,6},{8,9},{9,8},{10,11... | collective-permute-start | bytes 344072 | tf_op jit(solution)/shard_map/ppermute | solution.py:440
  31.3 0.0 collective-permute-done.15.other_ref
  31.3 1.5 %collective-permute-done.16.refs_0_ = bf16[528,128]{1,0:T(8,128)(2,1)S(1)} collective-permute-done((bf16[528,128]{1,0:T(8,128)(2,1)S(1)}, bf16[528,128]{1,0:T(8,128)(2,1)S(1)}, u32[]{:S(2)}, u32[]{:S(2)}) %collective-permute-start.16) | collective-permute-done | bytes 135200 | tf_op jit(solution)/shard_map/ppermute | solution.py:440
  32.9 1.4 %collective-permute-start.17 = (bf16[528,128]{1,0:T(8,128)(2,1)S(1)}, bf16[528,128]{1,0:T(8,128)(2,1)S(1)}, u32[]{:S(2)}, u32[]{:S(2)}) collective-permute-start(bf16[528,128]{1,0:T(8,128)(2,1)S(1)} %get-tuple-element.198), channel_id=1, source_target_pairs={{0,2},{1,3},{2,0},{3,1},{4,6},{5,7},{6,4},{7,5},{8,10},{9,11},{10,... | collective-permute-start | bytes 405512 | tf_op jit(solution)/shard_map/ppermute | solution.py:440
  34.3 1.7 %collective-permute-done.12.other_ref = bf16[448,128]{1,0:T(8,128)(2,1)S(1)} collective-permute-done((bf16[448,128]{1,0:T(8,128)(2,1)S(1)}, bf16[448,128]{1,0:T(8,128)(2,1)S(1)}, u32[]{:S(2)}, u32[]{:S(2)}) %collective-permute-start.12) | collective-permute-done | bytes 114720 | tf_op jit(solution)/shard_map/ppermute | solution.py:440
  36.0 1.2 %collective-permute-start.13 = (bf16[448,128]{1,0:T(8,128)(2,1)S(1)}, bf16[448,128]{1,0:T(8,128)(2,1)S(1)}, u32[]{:S(2)}, u32[]{:S(2)}) collective-permute-start(bf16[448,128]{1,0:T(8,128)(2,1)S(1)} %get-tuple-element.190), channel_id=1, source_target_pairs={{0,2},{1,3},{2,0},{3,1},{4,6},{5,7},{6,4},{7,5},{8,10},{9,11},{10,... | collective-permute-start | bytes 344072 | tf_op jit(solution)/shard_map/ppermute | solution.py:440
  37.2 1.7 %collective-permute-start.14 = (bf16[448,128]{1,0:T(8,128)(2,1)S(1)}, bf16[448,128]{1,0:T(8,128)(2,1)}, u32[]{:S(2)}, u32[]{:S(2)}) collective-permute-start(bf16[448,128]{1,0:T(8,128)(2,1)S(1)} %get-tuple-element.191), channel_id=1, source_target_pairs={{0,1},{1,0},{2,3},{3,2},{4,5},{5,4},{6,7},{7,6},{8,9},{9,8},{10,11... | collective-permute-start | bytes 344072 | tf_op jit(solution)/shard_map/ppermute | solution.py:440
  39.0 4.8 %input_grad.1 = bf16[2,288,680]{2,1,0:T(8,128)(2,1)} custom-call(s32[1]{0:T(128)} %bitcast.3.me_ref, f32[2,680]{1,0:T(2,128)S(1)} %get-tuple-element.172.refs_4_.other_token_ref.refs_3_.mean_ref, f32[2,680]{1,0:T(2,128)S(1)} %get-tuple-element.173.inverse_ref, bf16[360,360]{1,0:T(8,128)(2,1)S(1)} %get-tuple-element.174.same_group_ref, ...), custom_call_target="tpu_custom_call" | custom-call | flops 532684800 | bytes 3133440 | tf_op jit(solution)/shard_map/input_grad/pallas_call | solution.py:418
  43.8 0.0 collective-permute-done.17.refs_1_
  43.8 0.9 %adam.7 = (f32[176,360]{1,0:T(8,128)S(1)}, f32[176,360]{1,0:T(8,128)S(1)}, bf16[528,128]{1,0:T(8,128)(2,1)S(1)}) custom-call(f32[4]{0:T(128)S(1)} %pad_maximum_fusion.scales_ref, f32[176,360]{1,0:T(8,128)S(1)} %get-tuple-element.182.refs_4_.own_ref, bf16[528,128]{1,0:T(8,128)(2,1)S(1)} %get-tuple-element.197.refs_0_, ...), custom_call_target="tpu_custom_call" | custom-call | bytes 489600 | tf_op jit(solution)/shard_map/adam/pallas_call | solution.py:418
  44.7 0.2 collective-permute-done.13
  44.9 0.0 collective-permute-done.14
  45.0 8.7 %conditional.1 = (f32[170,1,680]{2,1,0:T(1,128)}, f32[170,1,680]{2,1,0:T(1,128)}, f32[1]{0:T(128)}, f32[1,170,680]{2,0,1:T(1,128)}) conditional(s32[]{:T(128)} %clamp.3, (f32[4]{0:T(128)S(1)}, f32[176,320]{1,0:T(8,128)S(1)}, bf16[448,128]{1,0:T(8,128)(2,1)S(1)}, bf16[448,128]{1,0:T(8,128)(2,1)}, f32[170,320]{1,0:T(8,128)S(1)}, ...), branch_computations={%region_0.1_spmd, %region_1.2_spmd, %region_2.3_spmd} | conditional | bytes 3773936 | solution.py:633
  45.0 1.6 %collective-permute-start.4 = (bf16[528,128]{1,0:T(8,128)(2,1)S(1)}, bf16[528,128]{1,0:T(8,128)(2,1)S(1)}, u32[]{:S(2)}, u32[]{:S(2)}) collective-permute-start(bf16[528,128]{1,0:T(8,128)(2,1)S(1)} %get-tuple-element.125), channel_id=1, source_target_pairs={{0,16},{4,20},{8,24},{12,28},{16,0},{20,4},{24,8},{28,12},{1,17},{... | collective-permute-start | bytes 405512 | tf_op jit(solution)/shard_map/cond/branch_2_fun/ppermute | solution.py:436
  46.6 1.3 %adam.6 = (f32[176,320]{1,0:T(8,128)S(1)}, f32[176,320]{1,0:T(8,128)S(1)}, bf16[448,128]{1,0:T(8,128)(2,1)S(1)}) custom-call(f32[4]{0:T(128)S(1)} %get-tuple-element.114.scales_ref, f32[176,320]{1,0:T(8,128)S(1)} %get-tuple-element.115.own_ref, bf16[448,128]{1,0:T(8,128)(2,1)S(1)} %get-tuple-element.116.refs_0_, ...), custom_call_target="tpu_custom_call" | custom-call | bytes 435200 | tf_op jit(solution)/shard_map/cond/branch_2_fun/adam/pallas_call | solution.py:418
  47.9 0.6 %collective-permute-start.5 = (bf16[448,128]{1,0:T(8,128)(2,1)S(1)}, bf16[448,128]{1,0:T(8,128)(2,1)S(1)}, u32[]{:S(2)}, u32[]{:S(2)}) collective-permute-start(bf16[448,128]{1,0:T(8,128)(2,1)S(1)} %get-tuple-element.129), channel_id=1, source_target_pairs={{0,16},{4,20},{8,24},{12,28},{16,0},{20,4},{24,8},{28,12},{1,17},{... | collective-permute-start | bytes 344072 | tf_op jit(solution)/shard_map/cond/branch_2_fun/ppermute | solution.py:436
  48.4 2.4 %moments.5 = (f32[170,1,680]{2,1,0:T(1,128)}, f32[170,1,680]{2,1,0:T(1,128)}) custom-call(f32[170,1,680]{2,1,0:T(1,128)} %get-tuple-element.111.first_hbm, f32[170,1,680]{2,1,0:T(1,128)} %get-tuple-element.112.second_hbm, f32[176,360]{1,0:T(8,128)S(1)} %get-tuple-element.113.refs_0_, f32[176,320]{1,0:T(8,128)S(1)} %get-tuple-element.121.refs_1_), custom_call_target="tpu_custom_call" | custom-call | bytes 924800 | tf_op jit(solution)/shard_map/cond/branch_2_fun/moments/pallas_call | solution.py:418
  50.9 0.4 collective-permute-done.4.other_ref
  51.3 1.1 %half_average.5 = (f32[176,360]{1,0:T(8,128)S(1)}, f32[1]{0:T(128)}) custom-call(f32[4]{0:T(128)S(1)} %get-tuple-element.114.scales_ref, f32[176,360]{1,0:T(8,128)S(1)} %get-tuple-element.124.moved_ref, bf16[528,128]{1,0:T(8,128)(2,1)S(1)} %collective-permute-done.4.other_ref), custom_call_target="tpu_custom_call" | custom-call | bytes 489600 | tf_op jit(solution)/shard_map/cond/branch_2_fun/half_average/pallas_call | solution.py:418
  52.4 0.4 collective-permute-done.5.other_ref
  52.7 1.0 %average.5 = f32[170,1,680]{2,1,0:T(1,128)} custom-call(f32[176,360]{1,0:T(8,128)S(1)} %get-tuple-element.127.mean_ref, f32[176,320]{1,0:T(8,128)S(1)} %get-tuple-element.128.moved_ref, bf16[448,128]{1,0:T(8,128)(2,1)S(1)} %collective-permute-done.5.other_ref), custom_call_target="tpu_custom_call" | custom-call | bytes 924800 | tf_op jit(solution)/shard_map/cond/branch_2_fun/average/pallas_call | solution.py:418
  (19 shorter events, 0.1 us)
Async XLA Ops:
  1.3 1.0 %copy-start = (f32[1,170,680]{2,0,1:T(1,128)S(1)}, f32[1,170,680]{2,0,1:T(1,128)}, u32[]{:S(2)}) copy-start(f32[1,170,680]{2,0,1:T(1,128)} %param.14) | copy-start | bytes 1387204
  2.5 10.5 %collective-permute-start.6 = (bf16[528,128]{1,0:T(8,128)(2,1)S(1)}, bf16[528,128]{1,0:T(8,128)(2,1)S(1)}, u32[]{:S(2)}, u32[]{:S(2)}) collective-permute-start(bf16[528,128]{1,0:T(8,128)(2,1)S(1)} %cast.2.refs_0_), channel_id=1, source_target_pairs={{0,1},{1,0},{2,3},{3,2},{4,5},{5,4},{6,7},{7,6},{8,9},{9,8},{10,11... | collective-permute-start | bytes 405512 | tf_op jit(solution)/shard_map/ppermute | solution.py:440
  5.6 8.9 %collective-permute-start.7 = (bf16[528,128]{1,0:T(8,128)(2,1)S(1)}, bf16[528,128]{1,0:T(8,128)(2,1)S(1)}, u32[]{:S(2)}, u32[]{:S(2)}) collective-permute-start(bf16[528,128]{1,0:T(8,128)(2,1)S(1)} %cast.2.refs_0_), channel_id=1, source_target_pairs={{0,2},{1,3},{2,0},{3,1},{4,6},{5,7},{6,4},{7,5},{8,10},{9,11},{10,... | collective-permute-start | bytes 405512 | tf_op jit(solution)/shard_map/ppermute | solution.py:440
  9.0 0.7 %copy-start.7 = (bf16[2,680]{1,0:T(2,128)(2,1)S(1)}, bf16[2,680]{1,0:T(2,128)(2,1)}, u32[]{:S(2)}) copy-start(bf16[2,680]{1,0:T(2,128)(2,1)} %shift_ref.1) | copy-start | bytes 8164
  9.7 3.4 %copy-start.1 = (f32[1,170,680]{2,0,1:T(1,128)S(1)}, f32[1,170,680]{2,0,1:T(1,128)}, u32[]{:S(2)}) copy-start(f32[1,170,680]{2,0,1:T(1,128)} %param.14) | copy-start | bytes 1387204
  13.3 7.7 %collective-permute-start.10 = (bf16[448,128]{1,0:T(8,128)(2,1)S(1)}, bf16[448,128]{1,0:T(8,128)(2,1)S(1)}, u32[]{:S(2)}, u32[]{:S(2)}) collective-permute-start(bf16[448,128]{1,0:T(8,128)(2,1)S(1)} %cast.3.refs_0_), channel_id=1, source_target_pairs={{0,2},{1,3},{2,0},{3,1},{4,6},{5,7},{6,4},{7,5},{8,10},{9,11},{10,... | collective-permute-start | bytes 344072 | tf_op jit(solution)/shard_map/ppermute | solution.py:440
  14.5 7.9 %collective-permute-start.8 = (bf16[528,128]{1,0:T(8,128)(2,1)S(1)}, bf16[528,128]{1,0:T(8,128)(2,1)S(1)}, u32[]{:S(2)}, u32[]{:S(2)}) collective-permute-start(bf16[528,128]{1,0:T(8,128)(2,1)S(1)} %collective-permute-done.7.refs_2_), channel_id=1, source_target_pairs={{0,1},{1,0},{2,3},{3,2},{4,5},{5,4},{6,7},{7,6},{8,9},{9,8},{10,11... | collective-permute-start | bytes 405512 | tf_op jit(solution)/shard_map/ppermute | solution.py:440
  18.0 9.2 %collective-permute-start.9 = (bf16[448,128]{1,0:T(8,128)(2,1)S(1)}, bf16[448,128]{1,0:T(8,128)(2,1)S(1)}, u32[]{:S(2)}, u32[]{:S(2)}) collective-permute-start(bf16[448,128]{1,0:T(8,128)(2,1)S(1)} %cast.3.refs_0_), channel_id=1, source_target_pairs={{0,1},{1,0},{2,3},{3,2},{4,5},{5,4},{6,7},{7,6},{8,9},{9,8},{10,11... | collective-permute-start | bytes 344072 | tf_op jit(solution)/shard_map/ppermute | solution.py:440
  21.1 6.1 %collective-permute-start.11 = (bf16[448,128]{1,0:T(8,128)(2,1)S(1)}, bf16[448,128]{1,0:T(8,128)(2,1)S(1)}, u32[]{:S(2)}, u32[]{:S(2)}) collective-permute-start(bf16[448,128]{1,0:T(8,128)(2,1)S(1)} %hold.1.refs_2_), channel_id=1, source_target_pairs={{0,1},{1,0},{2,3},{3,2},{4,5},{5,4},{6,7},{7,6},{8,9},{9,8},{10,11... | collective-permute-start | bytes 344072 | tf_op jit(solution)/shard_map/ppermute | solution.py:440
  25.1 6.2 %collective-permute-start.15 = (bf16[528,128]{1,0:T(8,128)(2,1)S(1)}, bf16[528,128]{1,0:T(8,128)(2,1)S(1)}, u32[]{:S(2)}, u32[]{:S(2)}) collective-permute-start(bf16[528,128]{1,0:T(8,128)(2,1)S(1)} %get-tuple-element.195), channel_id=1, source_target_pairs={{0,1},{1,0},{2,3},{3,2},{4,5},{5,4},{6,7},{7,6},{8,9},{9,8},{10,11... | collective-permute-start | bytes 405512 | tf_op jit(solution)/shard_map/ppermute | solution.py:440
  26.0 6.8 %collective-permute-start.16 = (bf16[528,128]{1,0:T(8,128)(2,1)S(1)}, bf16[528,128]{1,0:T(8,128)(2,1)S(1)}, u32[]{:S(2)}, u32[]{:S(2)}) collective-permute-start(bf16[528,128]{1,0:T(8,128)(2,1)S(1)} %get-tuple-element.196), channel_id=1, source_target_pairs={{0,1},{1,0},{2,3},{3,2},{4,5},{5,4},{6,7},{7,6},{8,9},{9,8},{10,11... | collective-permute-start | bytes 405512 | tf_op jit(solution)/shard_map/ppermute | solution.py:440
  27.2 11.8 %copy-start.3 = (bf16[576,360]{1,0:T(8,128)(2,1)S(1)}, bf16[576,360]{1,0:T(8,128)(2,1)}, u32[]{:S(2)}) copy-start(bf16[576,360]{1,0:T(8,128)(2,1)} %get-tuple-element.178.refs_0_) | copy-start | bytes 1244164
  30.4 8.6 %copy-start.2 = (bf16[704,360]{1,0:T(8,128)(2,1)S(1)}, bf16[704,360]{1,0:T(8,128)(2,1)}, u32[]{:S(2)}) copy-start(bf16[704,360]{1,0:T(8,128)(2,1)} %get-tuple-element.184.refs_2_) | copy-start | bytes 1520644
  30.4 5.6 %collective-permute-start.12 = (bf16[448,128]{1,0:T(8,128)(2,1)S(1)}, bf16[448,128]{1,0:T(8,128)(2,1)S(1)}, u32[]{:S(2)}, u32[]{:S(2)}) collective-permute-start(bf16[448,128]{1,0:T(8,128)(2,1)S(1)} %get-tuple-element.188), channel_id=1, source_target_pairs={{0,1},{1,0},{2,3},{3,2},{4,5},{5,4},{6,7},{7,6},{8,9},{9,8},{10,11... | collective-permute-start | bytes 344072 | tf_op jit(solution)/shard_map/ppermute | solution.py:440
  32.9 10.9 %collective-permute-start.17 = (bf16[528,128]{1,0:T(8,128)(2,1)S(1)}, bf16[528,128]{1,0:T(8,128)(2,1)S(1)}, u32[]{:S(2)}, u32[]{:S(2)}) collective-permute-start(bf16[528,128]{1,0:T(8,128)(2,1)S(1)} %get-tuple-element.198), channel_id=1, source_target_pairs={{0,2},{1,3},{2,0},{3,1},{4,6},{5,7},{6,4},{7,5},{8,10},{9,11},{10,... | collective-permute-start | bytes 405512 | tf_op jit(solution)/shard_map/ppermute | solution.py:440
  36.0 8.9 %collective-permute-start.13 = (bf16[448,128]{1,0:T(8,128)(2,1)S(1)}, bf16[448,128]{1,0:T(8,128)(2,1)S(1)}, u32[]{:S(2)}, u32[]{:S(2)}) collective-permute-start(bf16[448,128]{1,0:T(8,128)(2,1)S(1)} %get-tuple-element.190), channel_id=1, source_target_pairs={{0,2},{1,3},{2,0},{3,1},{4,6},{5,7},{6,4},{7,5},{8,10},{9,11},{10,... | collective-permute-start | bytes 344072 | tf_op jit(solution)/shard_map/ppermute | solution.py:440
  37.2 7.7 %collective-permute-start.14 = (bf16[448,128]{1,0:T(8,128)(2,1)S(1)}, bf16[448,128]{1,0:T(8,128)(2,1)}, u32[]{:S(2)}, u32[]{:S(2)}) collective-permute-start(bf16[448,128]{1,0:T(8,128)(2,1)S(1)} %get-tuple-element.191), channel_id=1, source_target_pairs={{0,1},{1,0},{2,3},{3,2},{4,5},{5,4},{6,7},{7,6},{8,9},{9,8},{10,11... | collective-permute-start | bytes 344072 | tf_op jit(solution)/shard_map/ppermute | solution.py:440
  39.0 4.8 %copy-start.4 = (f32[170,360]{1,0:T(8,128)S(1)}, f32[170,360]{1,0:T(8,128)}, u32[]{:S(2)}) copy-start(f32[170,360]{1,0:T(8,128)} %get-tuple-element.199.refs_2_) | copy-start | bytes 734404
  39.0 4.8 %copy-start.5 = (f32[170,360]{1,0:T(8,128)S(1)}, f32[170,360]{1,0:T(8,128)}, u32[]{:S(2)}) copy-start(f32[170,360]{1,0:T(8,128)} %get-tuple-element.200.refs_3_) | copy-start | bytes 734404
  39.0 4.8 %copy-start.6 = (f32[170,360]{1,0:T(8,128)S(1)}, f32[170,360]{1,0:T(8,128)}, u32[]{:S(2)}) copy-start(f32[170,360]{1,0:T(8,128)} %get-tuple-element.201.refs_4_) | copy-start | bytes 734404
  43.8 1.1 %copy-start.8 = (f32[170,320]{1,0:T(8,128)S(1)}, f32[170,320]{1,0:T(8,128)}, u32[]{:S(2)}) copy-start(f32[170,320]{1,0:T(8,128)} %get-tuple-element.181.token_ref) | copy-start | bytes 652804
  43.8 1.1 %copy-start.9 = (f32[170,320]{1,0:T(8,128)S(1)}, f32[170,320]{1,0:T(8,128)}, u32[]{:S(2)}) copy-start(f32[170,320]{1,0:T(8,128)} %get-tuple-element.192) | copy-start | bytes 652804
  43.8 1.1 %copy-start.10 = (f32[170,320]{1,0:T(8,128)S(1)}, f32[170,320]{1,0:T(8,128)}, u32[]{:S(2)}) copy-start(f32[170,320]{1,0:T(8,128)} %get-tuple-element.193) | copy-start | bytes 652804
  45.0 6.3 %collective-permute-start.4 = (bf16[528,128]{1,0:T(8,128)(2,1)S(1)}, bf16[528,128]{1,0:T(8,128)(2,1)S(1)}, u32[]{:S(2)}, u32[]{:S(2)}) collective-permute-start(bf16[528,128]{1,0:T(8,128)(2,1)S(1)} %get-tuple-element.125), channel_id=1, source_target_pairs={{0,16},{4,20},{8,24},{12,28},{16,0},{20,4},{24,8},{28,12},{1,17},{... | collective-permute-start | bytes 405512 | tf_op jit(solution)/shard_map/cond/branch_2_fun/ppermute | solution.py:436
  47.9 4.9 %collective-permute-start.5 = (bf16[448,128]{1,0:T(8,128)(2,1)S(1)}, bf16[448,128]{1,0:T(8,128)(2,1)S(1)}, u32[]{:S(2)}, u32[]{:S(2)}) collective-permute-start(bf16[448,128]{1,0:T(8,128)(2,1)S(1)} %get-tuple-element.129), channel_id=1, source_target_pairs={{0,16},{4,20},{8,24},{12,28},{16,0},{20,4},{24,8},{28,12},{1,17},{... | collective-permute-start | bytes 344072 | tf_op jit(solution)/shard_map/cond/branch_2_fun/ppermute | solution.py:436
where the time goes:
time: 53.5 us; the launch traced here: 53.7 us
  Pallas kernels  23.7 us (44%)
  starting transfers between devices  17.7 us (33%)
  waiting for transfers between devices  8.26 us (15%)
  between operations  2.3 us (4%)
  local copies, waits for them, and re-layouts  1.63 us (3%)
    pallas_call x15, Pallas kernels, call(): pl.pallas_call(kernel, out_shape=outs, in_specs=specs, out_specs=out_spec...  23.7 us
    ppermute x12, starting transfers between devices, exchanged(): lax.ppermute(block, axis, [(i, i ^ bit) for i in range(lax.axis_size(axis...  15.6 us
    ppermute x12, waiting for transfers between devices, exchanged(): lax.ppermute(block, axis, [(i, i ^ bit) for i in range(lax.axis_size(axis...  7.49 us
    ppermute x2, starting transfers between devices, moved_on(): lax.ppermute(block, axis, [(i, (i + distance) % size) for i in range(size)])  2.16 us
    unnamed x22, local copies, waits for them, and re-layouts  1.63 us
  transfers between devices with their start and end apart: 14, of which 8 were waited for; matrix products, arithmetic and copies ran while one was open for 0% of the time, Pallas kernels for 42%

commit v1 on v0

--- a/solution.py
+++ b/solution.py
@@ -143,7 +143,7 @@
     return jnp.concatenate(sums, axis=0)
 
 
-def norm_back(table_mean, samples, positions, step, load, scales, offsets, inverse, incoming, kept_ref, store):
+def norm_back(table_mean, samples, positions, step, load, scales, offsets, inverse, incoming, kept_ref, store, stored):
     firsts, seconds = [], []
     zeros = jnp.zeros((8, scales.shape[1]), jnp.float32)
     for i in range(samples):
@@ -173,6 +173,7 @@
             return carry
 
         lax.fori_loop(0, positions // step, body, 0, unroll=UNROLL)
+        stored(i)
 
 
 def sigmoid(values):
@@ -232,10 +233,11 @@
             out_grad_out[i] = out_grad_ref[i][:, pack.start : pack.stop]
 
 
-def mix_kernel(shards, pack, act_ref, shift_ref, out_grad_ref, same_group_ref, *refs):
+def mix_kernel(shards, pack, slots, act_ref, shift_ref, out_grad_ref, same_group_ref, *refs):
     weight_refs, token_ref, refs = refs[:shards], refs[shards], refs[shards + 1 :]
-    grad_hidden_ref, weight_out_ref, own_ref = refs[:3]
-    send_refs, (weight_ref, kept_ref, hidden_ref, doubled_ref, sems) = refs[3 : 2 + shards], refs[2 + shards :]
+    grad_hidden_ref, weight_out_ref = refs[:2]
+    made_refs, refs = refs[2 : 2 + len(slots)], refs[2 + len(slots) :]
+    weight_ref, kept_ref, hidden_ref, doubled_ref, sems = refs
     samples, positions, columns = out_grad_ref.shape
     entries = positions * GSIZE
     deep = pack.deep
@@ -267,24 +269,44 @@
     inverse = lax.rsqrt(table_mean(squares) + NORM_EPS)
     scales = 0.5 * inverse
     norm_back(
-        table_mean, samples, positions, ROW_STEP, load, scales, offset * scales, inverse, incoming, doubled_ref, store
+        table_mean, samples, positions, ROW_STEP, load, scales, offset * scales, inverse, incoming, doubled_ref, store, lambda i: None
     )
     copy = pltpu.make_async_copy(kept_ref, grad_hidden_ref, sems.at[1])
     copy.start()
-    grad = jnp.dot(act_ref[...], kept_ref[...], preferred_element_type=jnp.float32)
-    for slot, send_ref in enumerate(send_refs, 1):
-        pack.write(send_ref, grad[slot * deep : (slot + 1) * deep])
-    own_ref[...] = grad[:deep]
+    weight_grads(pack, slots, act_ref, kept_ref, made_refs)
     weight_copy.wait()
     copy.wait()
 
 
-def input_grad_kernel(shards, packs, me_ref, mean_ref, inverse_ref, same_group_ref, x_hbm, *refs):
+def weight_grads(pack, slots, act_ref, grad_hidden_ref, made_refs):
+    deep = pack.deep
+    low, high = min(slots), max(slots) + 1
+    grad = jnp.dot(act_ref[low * deep : high * deep, :], grad_hidden_ref[...], preferred_element_type=jnp.float32)
+    for slot, made_ref in zip(slots, made_refs):
+        block = grad[(slot - low) * deep : (slot - low + 1) * deep]
+        if slot:
+            pack.write(made_ref, block)
+        else:
+            made_ref[...] = block
+
+
+def rest_kernel(pack, slots, act_ref, grad_hidden_ref, token_ref, *made_refs):
+    weight_grads(pack, slots, act_ref, grad_hidden_ref, made_refs)
+
+
+def input_grad_kernel(shards, packs, carried, me_ref, mean_ref, inverse_ref, same_group_ref, x_hbm, *refs):
     count = len(packs)
-    grad_refs, weight_refs, out_ref = refs[:count], refs[count : 2 * count], refs[2 * count]
-    rows_ref, x_ref, made_ref, act_ref, sems = refs[2 * count + 1 :]
+    grad_refs, weight_refs, refs = refs[:count], refs[count : 2 * count], refs[2 * count :]
+    carried_hbms, out_ref, carried_refs = refs[:carried], refs[carried], refs[carried + 1 : 2 * carried + 1]
+    rows_ref, x_ref, made_ref, act_ref, sems, carried_sems = refs[2 * carried + 1 :]
     copies = [pltpu.make_async_copy(x_hbm, x_ref, sems.at[0])]
     copies[0].start()
+    carried_copies = [
+        pltpu.make_async_copy(source, target, carried_sems.at[i])
+        for i, (source, target) in enumerate(zip(carried_hbms, carried_refs))
+    ]
+    for copy in carried_copies:
+        copy.start()
     samples, positions, channels = x_ref.shape
     entries = positions * GSIZE
     rows = channels // shards
@@ -294,8 +316,8 @@
             slot = jnp.bitwise_xor(me_ref[0], block)
             rows_ref[block * rows : (block + 1) * rows, : pack.columns] = weight_ref[
                 pl.ds(pl.multiple_of(slot * pack.deep, TILE_ROWS), pack.deep), :
-            ].astype(jnp.float32)[:rows]
-        weights.append(rows_ref[:, : pack.columns].astype(jnp.bfloat16))
+            ][:rows]
+        weights.append(rows_ref[:, : pack.columns])
     grad_act = 0.0
     for index, (grad_ref, weight) in enumerate(zip(grad_refs, weights)):
         grad_act += lax.dot_general(
@@ -318,19 +340,20 @@
     def store(i, first_row, count, grad):
         made_ref[i, pl.ds(first_row, count), :] = grad.astype(jnp.bfloat16)
 
+    def stored(i):
+        copies.append(pltpu.make_async_copy(made_ref.at[i], out_ref.at[i], sems.at[len(copies)]))
+        copies[-1].start()
+
     scales = 0.5 * inverse
     norm_back(
-        table_mean, samples, positions, ROW_STEP, load, scales, -mean_ref[...] * scales, inverse, incoming, act_ref, store
-    )
-    for i in range(samples):
-        copies.append(pltpu.make_async_copy(made_ref.at[i], out_ref.at[i], sems.at[len(copies)]))
-        copies[-1].start()
-    for copy in copies[-samples:]:
+        table_mean, samples, positions, ROW_STEP // 2, load, scales, -mean_ref[...] * scales, inverse, incoming, act_ref, store, stored
+    )
+    for copy in carried_copies + copies[-samples:]:
         copy.wait()
 
 
 def merge_kernel(one_ref, other_ref, *refs):
-    count = len(refs) // 2
+    count = (len(refs) - 1) // 2
     through_refs, out_ref, through_out_refs = refs[:count], refs[count], refs[count + 1 :]
     out_ref[...] = (one_ref[...].astype(jnp.float32) + other_ref[...].astype(jnp.float32)).astype(out_ref.dtype)
     for through_ref, through_out_ref in zip(through_refs, through_out_refs):
@@ -460,11 +483,10 @@
 
 
 def scattered(parts, shards):
-    arrived = []
-    for part, sends in enumerate(parts):
-        held = dict(enumerate(sends, 1))
+    arrived, token = [], None
+    for part, held in enumerate(parts):
+        last = part == len(parts) - 1
         slots = sorted(range(2, shards), key=lambda slot: (-slot.bit_count(), -slot))
-        last = part == len(parts) - 1
         got = [] if last else [exchanged(held[1], "dp", 1)]
         for slot in slots:
             bit = lowest_bit(slot)
@@ -472,14 +494,24 @@
             if slot == bit:
                 got.append(other)
                 continue
+            if None in held:
+                held.update(held.pop(None)(token))
             shape = jax.ShapeDtypeStruct(other.shape, other.dtype)
-            held[slot ^ bit], held[1] = call(
-                merge_kernel, "merge", (shape,) * 2, [BLOCKS] * 3, (held[slot ^ bit], other, held[1] if last else got[0])
+            through = [held[1]] if last else []
+            made = call(
+                merge_kernel,
+                "merge",
+                (shape,) * (1 + len(through)),
+                [BLOCKS] * (2 + len(through)),
+                (held[slot ^ bit], other, *through),
             )
+            held[slot ^ bit] = made[0]
+            if last:
+                held[1] = made[1]
         if last:
             got.append(exchanged(held[1], "dp", 1))
         else:
-            got[0] = held[1]
+            token = got[0]
         arrived.append(got)
     return arrived
 
@@ -562,21 +594,23 @@
     )
     weights = [shards_of(packs[0], params, params)]
     weights.append(shards_of(packs[1], weights[0][1], mean_in, late=blocks[-1]))
-    hidden_grads, full_weights, owns, parts = [], [], [], []
+    hidden_grads, full_weights, parts = [], [], []
     token = mean_in
     shifts, out_grads = pieces[: len(packs)], pieces[len(packs) :]
     for pack, shard_list, shift, out_grad_piece in zip(packs, weights, shifts, out_grads):
         kept = jax.ShapeDtypeStruct if pack is packs[-1] else pltpu.HBM
         kept_spec = BLOCKS if pack is packs[-1] else IN_HBM
-        grad_hidden, full_weight, own, *sends = call(
-            functools.partial(mix_kernel, shards, pack),
+        later = range(shards - 1) if pack is packs[-1] and shards > 2 else range(0)
+        slots = [slot for slot in range(shards) if slot not in later]
+
+        def made(slots, pack=pack):
+            return tuple(pack.payload() if slot else pack.block() for slot in slots)
+
+        grad_hidden, full_weight, *shares = call(
+            functools.partial(mix_kernel, shards, pack, slots),
             "mix",
-            (
-                kept((tokens, pack.columns), jnp.bfloat16),
-                kept((shards * deep, pack.columns), jnp.bfloat16),
-                pack.block(),
-            )
-            + (pack.payload(),) * (shards - 1),
+            (kept((tokens, pack.columns), jnp.bfloat16), kept((shards * deep, pack.columns), jnp.bfloat16))
+            + made(slots),
             [BLOCKS] * (4 + shards) + [TOKEN],
             (activation, shift, out_grad_piece, same_group, *shard_list, token),
             scratch=[
@@ -586,31 +620,46 @@
                 pltpu.VMEM((tokens, pack.columns), jnp.float32),
                 pltpu.SemaphoreType.DMA((2,)),
             ],
-            out_specs=(kept_spec,) * 2 + (BLOCKS,) * shards,
+            out_specs=(kept_spec,) * 2 + (BLOCKS,) * len(slots),
             flops=4 * tokens * channels * pack.columns,
             elements=tokens * pack.columns,
         )
-        token = own
+        shares = dict(zip(slots, shares))
+        if later:
+            def rest(token, pack=pack, later=tuple(later), outs=made(later), grad_hidden=grad_hidden):
+                shares = call(
+                    functools.partial(rest_kernel, pack, later),
+                    "rest",
+                    outs,
+                    [BLOCKS] * 2 + [TOKEN],
+                    (activation, grad_hidden, token),
+                    flops=2 * tokens * channels * pack.columns,
+                )
+                return dict(zip(later, shares))
+
+            shares[None] = rest
+        token = shares[slots[-1]]
         hidden_grads.append(grad_hidden)
         full_weights.append(full_weight)
-        owns.append(own)
-        parts.append(sends)
-
-    def input_grad(*operands):
+        parts.append(shares)
+
+    def input_grad(carried, *operands):
         return call(
-            functools.partial(input_grad_kernel, shards, packs),
+            functools.partial(input_grad_kernel, shards, packs, len(carried)),
             "input_grad",
-            pltpu.HBM(block_input.shape, jnp.bfloat16),
-            [SCALARS] + [BLOCKS] * 3 + [IN_HBM] + [BLOCKS] * (2 * len(packs)),
-            operands[:4] + (stay(operands[4]),) + operands[5:],
+            (pltpu.HBM(block_input.shape, jnp.bfloat16),)
+            + tuple(jax.ShapeDtypeStruct(array.shape, array.dtype) for array in carried),
+            [SCALARS] + [BLOCKS] * 3 + [IN_HBM] + [BLOCKS] * (2 * len(packs)) + [IN_HBM] * len(carried),
+            operands[:4] + (stay(operands[4]),) + operands[5:] + tuple(map(stay, carried)),
             scratch=[
-                pltpu.VMEM((channels, max(pack.columns for pack in packs)), jnp.float32),
+                pltpu.VMEM((channels, max(pack.columns for pack in packs)), jnp.bfloat16),
                 pltpu.VMEM(block_input.shape, jnp.bfloat16),
                 pltpu.VMEM(block_input.shape, jnp.bfloat16),
                 pltpu.VMEM((tokens, channels), jnp.float32),
                 pltpu.SemaphoreType.DMA((1 + samples,)),
+                pltpu.SemaphoreType.DMA((len(carried),)),
             ],
-            out_specs=IN_HBM,
+            out_specs=(IN_HBM,) + (BLOCKS,) * len(carried),
             flops=2 * tokens * channels * channels,
             elements=tokens * channels,
         )
@@ -632,10 +681,11 @@
 
         return lax.switch(distance_bits, [branch(1 << power) for power in range(level_count)], *operands)
 
-    grad_input = input_grad(
-        me, mean_in, inverse_in, same_group, block_input, *hidden_grads, *full_weights
+    grad_input, *early_blocks = input_grad(
+        blocks[:3], me, mean_in, inverse_in, same_group, block_input, *hidden_grads, *full_weights
     )
     arrived = scattered(parts, shards)
+    owns = [shares[0] for shares in parts]
     early, late = packs
 
     def adam(pack, own, others, blocks):
@@ -648,7 +698,7 @@
             elements=rows * pack.columns,
         )
 
-    grad_a, moved_a, sent_a = adam(early, owns[0], arrived[0], blocks[:3])
+    grad_a, moved_a, sent_a = adam(early, owns[0], arrived[0], early_blocks)
 
     def finish(move, sent, grad_a, moved_a, own, *operands):
         other_a = move(sent)

time: 53.5 us -> 53.8 us (level)
    pallas_call x15 -> x16, Pallas kernels: 23.7 us -> 23.7 us  [call(): pl.pallas_call(kernel, out_shape=outs, in_specs=specs, out_specs=out_spec...]
    unnamed x22 -> x16, local copies, waits for them, and re-layouts: 1.63 us -> 1.62 us
  transfers between devices with their start and end apart: 14 -> 14, of which waited for: 8 -> 7; matrix products, arithmetic and copies ran while one was open for 0% -> 0% of each run, Pallas kernels for 42% -> 42%
where the time goes in v1:
time: 53.8 us; the launch traced here: 53.5 us
  Pallas kernels  23.7 us (44%)
  starting transfers between devices  17.7 us (33%)
  waiting for transfers between devices  8.03 us (15%)
  between operations  2.25 us (4%)
  local copies, waits for them, and re-layouts  1.62 us (3%)
    pallas_call x16, Pallas kernels, call(): pl.pallas_call(kernel, out_shape=outs, in_specs=specs, out_specs=out_spec...  23.7 us
    ppermute x12, starting transfers between devices, exchanged(): lax.ppermute(block, axis, [(i, i ^ bit) for i in range(lax.axis_size(axis...  15.6 us
    ppermute x12, waiting for transfers between devices, exchanged(): lax.ppermute(block, axis, [(i, i ^ bit) for i in range(lax.axis_size(axis...  7.27 us
    ppermute x2, starting transfers between devices, moved_on(): lax.ppermute(block, axis, [(i, (i + distance) % size) for i in range(size)])  2.16 us
    unnamed x16, local copies, waits for them, and re-layouts  1.62 us
  transfers between devices with their start and end apart: 14, of which 7 were waited for; matrix products, arithmetic and copies ran while one was open for 0% of the time, Pallas kernels for 42%

profile of v1, /device:TPU:0, one launch (start us, length us, event | category | flops | bytes accessed | tf_op | source)
XLA Modules:
  0.0 53.5 jit_solution(10863266309824383862)
XLA Ops:
  1.3 0.0 copy-start
  1.3 1.0 %copy-done = f32[1,170,680]{2,0,1:T(1,128)S(1)} copy-done((f32[1,170,680]{2,0,1:T(1,128)S(1)}, f32[1,170,680]{2,0,1:T(1,128)}, u32[]{:S(2)}) %copy-start) | copy-done | bytes 462424
  2.3 0.2 cast.2.refs_0_
  2.5 3.1 %collective-permute-start.6 = (bf16[528,128]{1,0:T(8,128)(2,1)S(1)}, bf16[528,128]{1,0:T(8,128)(2,1)S(1)}, u32[]{:S(2)}, u32[]{:S(2)}) collective-permute-start(bf16[528,128]{1,0:T(8,128)(2,1)S(1)} %cast.2.refs_0_), channel_id=1, source_target_pairs={{0,1},{1,0},{2,3},{3,2},{4,5},{5,4},{6,7},{7,6},{8,9},{9,8},{10,11... | collective-permute-start | bytes 405512 | tf_op jit(solution)/shard_map/ppermute | solution.py:463
  5.6 2.6 %collective-permute-start.7 = (bf16[528,128]{1,0:T(8,128)(2,1)S(1)}, bf16[528,128]{1,0:T(8,128)(2,1)S(1)}, u32[]{:S(2)}, u32[]{:S(2)}) collective-permute-start(bf16[528,128]{1,0:T(8,128)(2,1)S(1)} %cast.2.refs_0_), channel_id=1, source_target_pairs={{0,2},{1,3},{2,0},{3,1},{4,6},{5,7},{6,4},{7,5},{8,10},{9,11},{10,... | collective-permute-start | bytes 405512 | tf_op jit(solution)/shard_map/ppermute | solution.py:463
  9.0 0.0 copy-start.4
  9.0 0.1 pad_maximum_fusion.scales_ref
  9.1 0.6 %copy-done.4 = bf16[2,680]{1,0:T(2,128)(2,1)S(1)} copy-done((bf16[2,680]{1,0:T(2,128)(2,1)S(1)}, bf16[2,680]{1,0:T(2,128)(2,1)}, u32[]{:S(2)}) %copy-start.4) | copy-done | bytes 2744
  9.7 3.4 %norm_in.1 = (bf16[704,576]{1,0:T(8,128)(2,1)S(1)}, f32[2,680]{1,0:T(2,128)S(1)}, f32[2,680]{1,0:T(2,128)S(1)}, bf16[360,360]{1,0:T(8,128)(2,1)S(1)}, f32[2,360]...) custom-call(s32[1]{0:T(128)} %bitcast.3.me_ref, ...), custom_call_target="tpu_custom_call" | custom-call | bytes 3133440 | tf_op jit(solution)/shard_map/norm_in/pallas_call | solution.py:441
  13.0 0.0 collective-permute-done.6.refs_1_.token_ref
  13.0 0.0 copy-done.1
  13.0 0.3 cast.3.refs_0_
  13.3 0.4 collective-permute-start.10
  13.7 0.8 %collective-permute-done.7.refs_2_ = bf16[528,128]{1,0:T(8,128)(2,1)S(1)} collective-permute-done((bf16[528,128]{1,0:T(8,128)(2,1)S(1)}, bf16[528,128]{1,0:T(8,128)(2,1)S(1)}, u32[]{:S(2)}, u32[]{:S(2)}) %collective-permute-start.7) | collective-permute-done | bytes 135200 | tf_op jit(solution)/shard_map/ppermute | solution.py:463
  14.5 1.0 %collective-permute-start.8 = (bf16[528,128]{1,0:T(8,128)(2,1)S(1)}, bf16[528,128]{1,0:T(8,128)(2,1)S(1)}, u32[]{:S(2)}, u32[]{:S(2)}) collective-permute-start(bf16[528,128]{1,0:T(8,128)(2,1)S(1)} %collective-permute-done.7.refs_2_), channel_id=1, source_target_pairs={{0,1},{1,0},{2,3},{3,2},{4,5},{5,4},{6,7},{7,6},{8,9},{9,8},{10,11... | collective-permute-start | bytes 405512 | tf_op jit(solution)/shard_map/ppermute | solution.py:463
  15.5 2.4 %cut.1 = (f32[170,360]{1,0:T(8,128)}, f32[170,360]{1,0:T(8,128)}, f32[170,360]{1,0:T(8,128)}, f32[170,320]{1,0:T(8,128)}, f32[170,320]{1,0:T(8,128)}, /*index=5*/f32[170,320]{1,0:T(8,128)}) custom-call(f32[170,1,680]{2,1,0:T(1,128)} %bitcast.13, f32[170,1,680]{2,1,0:T(1,128)} %bitcast.18, f32[170,1,680]{2,1,0:T(1,128)} %bitcast.22, ...), custom_call_target="tpu_custom_call" | custom-call | bytes 924800 | tf_op jit(solution)/shard_map/cut/pallas_call | solution.py:441
  17.9 1.0 %collective-permute-start.9 = (bf16[448,128]{1,0:T(8,128)(2,1)S(1)}, bf16[448,128]{1,0:T(8,128)(2,1)S(1)}, u32[]{:S(2)}, u32[]{:S(2)}) collective-permute-start(bf16[448,128]{1,0:T(8,128)(2,1)S(1)} %cast.3.refs_0_), channel_id=1, source_target_pairs={{0,1},{1,0},{2,3},{3,2},{4,5},{5,4},{6,7},{7,6},{8,9},{9,8},{10,11... | collective-permute-start | bytes 344072 | tf_op jit(solution)/shard_map/ppermute | solution.py:463
  19.0 2.1 %collective-permute-done.10.block_ref = bf16[448,128]{1,0:T(8,128)(2,1)S(1)} collective-permute-done((bf16[448,128]{1,0:T(8,128)(2,1)S(1)}, bf16[448,128]{1,0:T(8,128)(2,1)S(1)}, u32[]{:S(2)}, u32[]{:S(2)}) %collective-permute-start.10) | collective-permute-done | bytes 114720 | tf_op jit(solution)/shard_map/ppermute | solution.py:463
  21.1 0.1 collective-permute-start.11
  21.2 1.2 %collective-permute-done.8.refs_3_ = bf16[528,128]{1,0:T(8,128)(2,1)S(1)} collective-permute-done((bf16[528,128]{1,0:T(8,128)(2,1)S(1)}, bf16[528,128]{1,0:T(8,128)(2,1)S(1)}, u32[]{:S(2)}, u32[]{:S(2)}) %collective-permute-start.8) | collective-permute-done | bytes 135200 | tf_op jit(solution)/shard_map/ppermute | solution.py:463
  22.3 2.8 %mix.2 = (bf16[576,360]{1,0:T(8,128)(2,1)}, bf16[704,360]{1,0:T(8,128)(2,1)}, f32[176,360]{1,0:T(8,128)S(1)}, bf16[528,128]{1,0:T(8,128)(2,1)S(1)}, bf16[528,128...) custom-call(bf16[704,576]{1,0:T(8,128)(2,1)S(1)} %get-tuple-element.177.act_ref, ...), custom_call_target="tpu_custom_call" | custom-call | flops 564019200 | bytes 1658880 | tf_op jit(solution)/shard_map/mix/pallas_call | solution.py:441
  25.1 0.9 %collective-permute-start.12 = (bf16[528,128]{1,0:T(8,128)(2,1)S(1)}, bf16[528,128]{1,0:T(8,128)(2,1)S(1)}, u32[]{:S(2)}, u32[]{:S(2)}) collective-permute-start(bf16[528,128]{1,0:T(8,128)(2,1)S(1)} %get-tuple-element.192), channel_id=1, source_target_pairs={{0,1},{1,0},{2,3},{3,2},{4,5},{5,4},{6,7},{7,6},{8,9},{9,8},{10,11... | collective-permute-start | bytes 405512 | tf_op jit(solution)/shard_map/ppermute | solution.py:463
  26.0 1.2 %collective-permute-start.16 = (bf16[528,128]{1,0:T(8,128)(2,1)S(1)}, bf16[528,128]{1,0:T(8,128)(2,1)S(1)}, u32[]{:S(2)}, u32[]{:S(2)}) collective-permute-start(bf16[528,128]{1,0:T(8,128)(2,1)S(1)} %get-tuple-element.184.refs_4_), channel_id=1, source_target_pairs={{0,1},{1,0},{2,3},{3,2},{4,5},{5,4},{6,7},{7,6},{8,9},{9,8},{10,11... | collective-permute-start | bytes 405512 | tf_op jit(solution)/shard_map/ppermute | solution.py:463
  27.2 0.0 collective-permute-done.9.refs_1_
  27.2 0.0 collective-permute-done.11.refs_3_
  27.2 2.8 %mix.3 = (bf16[576,320]{1,0:T(8,128)(2,1)S(1)}, bf16[704,320]{1,0:T(8,128)(2,1)S(1)}, bf16[448,128]{1,0:T(8,128)(2,1)S(1)}) custom-call(bf16[704,576]{1,0:T(8,128)(2,1)S(1)} %get-tuple-element.177.act_ref, f32[2,320]{1,0:T(2,128)S(1)} %get-tuple-element.181.shift_ref, bf16[2,288,320]{2,1,0:T(8,128)(2,1)S(1)} %get-tuple-element.182.out_grad_ref, ...), custom_call_target="tpu_custom_call" | custom-call | flops 501350400 | bytes 1474560 | tf_op jit(solution)/shard_map/mix/pallas_call | solution.py:441
  30.0 0.9 %collective-permute-start.13 = (bf16[448,128]{1,0:T(8,128)(2,1)S(1)}, bf16[448,128]{1,0:T(8,128)(2,1)S(1)}, u32[]{:S(2)}, u32[]{:S(2)}) collective-permute-start(bf16[448,128]{1,0:T(8,128)(2,1)S(1)} %get-tuple-element.195), channel_id=1, source_target_pairs={{0,1},{1,0},{2,3},{3,2},{4,5},{5,4},{6,7},{7,6},{8,9},{9,8},{10,11... | collective-permute-start | bytes 344072 | tf_op jit(solution)/shard_map/ppermute | solution.py:463
  30.9 2.3 %collective-permute-done.16.other_ref = bf16[528,128]{1,0:T(8,128)(2,1)S(1)} collective-permute-done((bf16[528,128]{1,0:T(8,128)(2,1)S(1)}, bf16[528,128]{1,0:T(8,128)(2,1)S(1)}, u32[]{:S(2)}, u32[]{:S(2)}) %collective-permute-start.16) | collective-permute-done | bytes 135200 | tf_op jit(solution)/shard_map/ppermute | solution.py:463
  33.2 1.4 %collective-permute-start.17 = (bf16[528,128]{1,0:T(8,128)(2,1)S(1)}, bf16[528,128]{1,0:T(8,128)(2,1)S(1)}, u32[]{:S(2)}, u32[]{:S(2)}) collective-permute-start(bf16[528,128]{1,0:T(8,128)(2,1)S(1)} %merge.3), channel_id=1, source_target_pairs={{0,2},{1,3},{2,0},{3,1},{4,6},{5,7},{6,4},{7,5},{8,10},{9,11},{10,... | collective-permute-start | bytes 405512 | tf_op jit(solution)/shard_map/ppermute | solution.py:463
  34.6 0.0 collective-permute-done.12.token_ref.refs_0_
  34.6 0.7 %rest.1 = (f32[176,320]{1,0:T(8,128)S(1)}, bf16[448,128]{1,0:T(8,128)(2,1)S(1)}, bf16[448,128]{1,0:T(8,128)(2,1)S(1)}) custom-call(bf16[704,576]{1,0:T(8,128)(2,1)S(1)} %get-tuple-element.177.act_ref, bf16[576,320]{1,0:T(8,128)(2,1)S(1)} %get-tuple-element.185.refs_1_.grad_hidden_ref, bf16[528,128]{1,0:T(8,128)(2,1)S(1)} %collective-permute-done.12.token_ref.refs_0_), custom_call_target="tpu_custom_call" | custom-call | flops 250675200 | tf_op jit(solution)/shard_map/rest/pallas_call | solution.py:441
  35.3 0.7 %collective-permute-done.13.other_ref = bf16[448,128]{1,0:T(8,128)(2,1)S(1)} collective-permute-done((bf16[448,128]{1,0:T(8,128)(2,1)S(1)}, bf16[448,128]{1,0:T(8,128)(2,1)S(1)}, u32[]{:S(2)}, u32[]{:S(2)}) %collective-permute-start.13) | collective-permute-done | bytes 114720 | tf_op jit(solution)/shard_map/ppermute | solution.py:463
  36.0 1.0 %collective-permute-start.14 = (bf16[448,128]{1,0:T(8,128)(2,1)S(1)}, bf16[448,128]{1,0:T(8,128)(2,1)S(1)}, u32[]{:S(2)}, u32[]{:S(2)}) collective-permute-start(bf16[448,128]{1,0:T(8,128)(2,1)S(1)} %get-tuple-element.197), channel_id=1, source_target_pairs={{0,2},{1,3},{2,0},{3,1},{4,6},{5,7},{6,4},{7,5},{8,10},{9,11},{10,... | collective-permute-start | bytes 344072 | tf_op jit(solution)/shard_map/ppermute | solution.py:463
  37.0 2.0 %collective-permute-start.15 = (bf16[448,128]{1,0:T(8,128)(2,1)S(1)}, bf16[448,128]{1,0:T(8,128)(2,1)}, u32[]{:S(2)}, u32[]{:S(2)}) collective-permute-start(bf16[448,128]{1,0:T(8,128)(2,1)S(1)} %get-tuple-element.198), channel_id=1, source_target_pairs={{0,1},{1,0},{2,3},{3,2},{4,5},{5,4},{6,7},{7,6},{8,9},{9,8},{10,11... | collective-permute-start | bytes 344072 | tf_op jit(solution)/shard_map/ppermute | solution.py:463
  39.0 4.5 %input_grad.1 = (bf16[2,288,680]{2,1,0:T(8,128)(2,1)}, f32[170,360]{1,0:T(8,128)S(1)}, f32[170,360]{1,0:T(8,128)S(1)}, f32[170,360]{1,0:T(8,128)S(1)}) custom-call(s32[1]{0:T(128)} %bitcast.3.me_ref, f32[2,680]{1,0:T(2,128)S(1)} %get-tuple-element.174.refs_4_.other_token_ref.refs_3_.mean_ref, f32[2,680]{1,0:T(2,128)S(1)} %get-tuple-element.175.inverse_ref, ...), custom_call_target="tpu_custom_call" | custom-call | flops 532684800 | bytes 3133440 | tf_op jit(solution)/shard_map/input_grad/pallas_call | solution.py:441
  43.5 0.0 collective-permute-done.17.refs_1_
  43.6 0.9 %adam.7 = (f32[176,360]{1,0:T(8,128)S(1)}, f32[176,360]{1,0:T(8,128)S(1)}, bf16[528,128]{1,0:T(8,128)(2,1)S(1)}) custom-call(f32[4]{0:T(128)S(1)} %pad_maximum_fusion.scales_ref, f32[176,360]{1,0:T(8,128)S(1)} %get-tuple-element.201.own_ref, bf16[528,128]{1,0:T(8,128)(2,1)S(1)} %collective-permute-done.12.token_ref.refs_0_, ...), custom_call_target="tpu_custom_call" | custom-call | bytes 489600 | tf_op jit(solution)/shard_map/adam/pallas_call | solution.py:441
  44.4 0.3 collective-permute-done.14
  44.7 0.0 collective-permute-done.15
  44.7 8.7 %conditional.1 = (f32[170,1,680]{2,1,0:T(1,128)}, f32[170,1,680]{2,1,0:T(1,128)}, f32[1]{0:T(128)}, f32[1,170,680]{2,0,1:T(1,128)}) conditional(s32[]{:T(128)} %clamp.3, (f32[4]{0:T(128)S(1)}, f32[176,320]{1,0:T(8,128)S(1)}, bf16[448,128]{1,0:T(8,128)(2,1)S(1)}, bf16[448,128]{1,0:T(8,128)(2,1)}, f32[170,320]{1,0:T(8,128)S(1)}, ...), branch_computations={%region_0.1_spmd, %region_1.2_spmd, %region_2.3_spmd} | conditional | bytes 3773936 | solution.py:682
  44.8 1.6 %collective-permute-start.4 = (bf16[528,128]{1,0:T(8,128)(2,1)S(1)}, bf16[528,128]{1,0:T(8,128)(2,1)S(1)}, u32[]{:S(2)}, u32[]{:S(2)}) collective-permute-start(bf16[528,128]{1,0:T(8,128)(2,1)S(1)} %get-tuple-element.125), channel_id=1, source_target_pairs={{0,16},{4,20},{8,24},{12,28},{16,0},{20,4},{24,8},{28,12},{1,17},{... | collective-permute-start | bytes 405512 | tf_op jit(solution)/shard_map/cond/branch_2_fun/ppermute | solution.py:459
  46.3 1.3 %adam.6 = (f32[176,320]{1,0:T(8,128)S(1)}, f32[176,320]{1,0:T(8,128)S(1)}, bf16[448,128]{1,0:T(8,128)(2,1)S(1)}) custom-call(f32[4]{0:T(128)S(1)} %get-tuple-element.114.scales_ref, f32[176,320]{1,0:T(8,128)S(1)} %get-tuple-element.115.own_ref, bf16[448,128]{1,0:T(8,128)(2,1)S(1)} %get-tuple-element.116.refs_0_, ...), custom_call_target="tpu_custom_call" | custom-call | bytes 435200 | tf_op jit(solution)/shard_map/cond/branch_2_fun/adam/pallas_call | solution.py:441
  47.6 0.6 %collective-permute-start.5 = (bf16[448,128]{1,0:T(8,128)(2,1)S(1)}, bf16[448,128]{1,0:T(8,128)(2,1)S(1)}, u32[]{:S(2)}, u32[]{:S(2)}) collective-permute-start(bf16[448,128]{1,0:T(8,128)(2,1)S(1)} %get-tuple-element.129), channel_id=1, source_target_pairs={{0,16},{4,20},{8,24},{12,28},{16,0},{20,4},{24,8},{28,12},{1,17},{... | collective-permute-start | bytes 344072 | tf_op jit(solution)/shard_map/cond/branch_2_fun/ppermute | solution.py:459
  48.2 2.4 %moments.5 = (f32[170,1,680]{2,1,0:T(1,128)}, f32[170,1,680]{2,1,0:T(1,128)}) custom-call(f32[170,1,680]{2,1,0:T(1,128)} %get-tuple-element.111.first_hbm, f32[170,1,680]{2,1,0:T(1,128)} %get-tuple-element.112.second_hbm, f32[176,360]{1,0:T(8,128)S(1)} %get-tuple-element.113.refs_0_, f32[176,320]{1,0:T(8,128)S(1)} %get-tuple-element.121.refs_1_), custom_call_target="tpu_custom_call" | custom-call | bytes 924800 | tf_op jit(solution)/shard_map/cond/branch_2_fun/moments/pallas_call | solution.py:441
  50.7 0.0 collective-permute-done.4.other_ref
  50.7 1.1 %half_average.5 = (f32[176,360]{1,0:T(8,128)S(1)}, f32[1]{0:T(128)}) custom-call(f32[4]{0:T(128)S(1)} %get-tuple-element.114.scales_ref, f32[176,360]{1,0:T(8,128)S(1)} %get-tuple-element.124.moved_ref, bf16[528,128]{1,0:T(8,128)(2,1)S(1)} %collective-permute-done.4.other_ref), custom_call_target="tpu_custom_call" | custom-call | bytes 489600 | tf_op jit(solution)/shard_map/cond/branch_2_fun/half_average/pallas_call | solution.py:441
  51.7 0.8 %collective-permute-done.5.other_ref = bf16[448,128]{1,0:T(8,128)(2,1)S(1)} collective-permute-done((bf16[448,128]{1,0:T(8,128)(2,1)S(1)}, bf16[448,128]{1,0:T(8,128)(2,1)S(1)}, u32[]{:S(2)}, u32[]{:S(2)}) %collective-permute-start.5) | collective-permute-done | bytes 114720 | tf_op jit(solution)/shard_map/cond/branch_2_fun/ppermute | solution.py:459
  52.5 1.0 %average.5 = f32[170,1,680]{2,1,0:T(1,128)} custom-call(f32[176,360]{1,0:T(8,128)S(1)} %get-tuple-element.127.mean_ref, f32[176,320]{1,0:T(8,128)S(1)} %get-tuple-element.128.moved_ref, bf16[448,128]{1,0:T(8,128)(2,1)S(1)} %collective-permute-done.5.other_ref), custom_call_target="tpu_custom_call" | custom-call | bytes 924800 | tf_op jit(solution)/shard_map/cond/branch_2_fun/average/pallas_call | solution.py:441
  (14 shorter events, 0.1 us)
Async XLA Ops:
  1.3 1.0 %copy-start = (f32[1,170,680]{2,0,1:T(1,128)S(1)}, f32[1,170,680]{2,0,1:T(1,128)}, u32[]{:S(2)}) copy-start(f32[1,170,680]{2,0,1:T(1,128)} %param.14) | copy-start | bytes 1387204
  2.5 10.5 %collective-permute-start.6 = (bf16[528,128]{1,0:T(8,128)(2,1)S(1)}, bf16[528,128]{1,0:T(8,128)(2,1)S(1)}, u32[]{:S(2)}, u32[]{:S(2)}) collective-permute-start(bf16[528,128]{1,0:T(8,128)(2,1)S(1)} %cast.2.refs_0_), channel_id=1, source_target_pairs={{0,1},{1,0},{2,3},{3,2},{4,5},{5,4},{6,7},{7,6},{8,9},{9,8},{10,11... | collective-permute-start | bytes 405512 | tf_op jit(solution)/shard_map/ppermute | solution.py:463
  5.6 8.9 %collective-permute-start.7 = (bf16[528,128]{1,0:T(8,128)(2,1)S(1)}, bf16[528,128]{1,0:T(8,128)(2,1)S(1)}, u32[]{:S(2)}, u32[]{:S(2)}) collective-permute-start(bf16[528,128]{1,0:T(8,128)(2,1)S(1)} %cast.2.refs_0_), channel_id=1, source_target_pairs={{0,2},{1,3},{2,0},{3,1},{4,6},{5,7},{6,4},{7,5},{8,10},{9,11},{10,... | collective-permute-start | bytes 405512 | tf_op jit(solution)/shard_map/ppermute | solution.py:463
  9.0 0.7 %copy-start.4 = (bf16[2,680]{1,0:T(2,128)(2,1)S(1)}, bf16[2,680]{1,0:T(2,128)(2,1)}, u32[]{:S(2)}) copy-start(bf16[2,680]{1,0:T(2,128)(2,1)} %shift_ref.1) | copy-start | bytes 8164
  9.7 3.4 %copy-start.1 = (f32[1,170,680]{2,0,1:T(1,128)S(1)}, f32[1,170,680]{2,0,1:T(1,128)}, u32[]{:S(2)}) copy-start(f32[1,170,680]{2,0,1:T(1,128)} %param.14) | copy-start | bytes 1387204
  13.3 7.7 %collective-permute-start.10 = (bf16[448,128]{1,0:T(8,128)(2,1)S(1)}, bf16[448,128]{1,0:T(8,128)(2,1)S(1)}, u32[]{:S(2)}, u32[]{:S(2)}) collective-permute-start(bf16[448,128]{1,0:T(8,128)(2,1)S(1)} %cast.3.refs_0_), channel_id=1, source_target_pairs={{0,2},{1,3},{2,0},{3,1},{4,6},{5,7},{6,4},{7,5},{8,10},{9,11},{10,... | collective-permute-start | bytes 344072 | tf_op jit(solution)/shard_map/ppermute | solution.py:463
  14.5 7.9 %collective-permute-start.8 = (bf16[528,128]{1,0:T(8,128)(2,1)S(1)}, bf16[528,128]{1,0:T(8,128)(2,1)S(1)}, u32[]{:S(2)}, u32[]{:S(2)}) collective-permute-start(bf16[528,128]{1,0:T(8,128)(2,1)S(1)} %collective-permute-done.7.refs_2_), channel_id=1, source_target_pairs={{0,1},{1,0},{2,3},{3,2},{4,5},{5,4},{6,7},{7,6},{8,9},{9,8},{10,11... | collective-permute-start | bytes 405512 | tf_op jit(solution)/shard_map/ppermute | solution.py:463
  17.9 9.3 %collective-permute-start.9 = (bf16[448,128]{1,0:T(8,128)(2,1)S(1)}, bf16[448,128]{1,0:T(8,128)(2,1)S(1)}, u32[]{:S(2)}, u32[]{:S(2)}) collective-permute-start(bf16[448,128]{1,0:T(8,128)(2,1)S(1)} %cast.3.refs_0_), channel_id=1, source_target_pairs={{0,1},{1,0},{2,3},{3,2},{4,5},{5,4},{6,7},{7,6},{8,9},{9,8},{10,11... | collective-permute-start | bytes 344072 | tf_op jit(solution)/shard_map/ppermute | solution.py:463
  21.1 6.1 %collective-permute-start.11 = (bf16[448,128]{1,0:T(8,128)(2,1)S(1)}, bf16[448,128]{1,0:T(8,128)(2,1)S(1)}, u32[]{:S(2)}, u32[]{:S(2)}) collective-permute-start(bf16[448,128]{1,0:T(8,128)(2,1)S(1)} %hold.1.refs_2_), channel_id=1, source_target_pairs={{0,1},{1,0},{2,3},{3,2},{4,5},{5,4},{6,7},{7,6},{8,9},{9,8},{10,11... | collective-permute-start | bytes 344072 | tf_op jit(solution)/shard_map/ppermute | solution.py:463
  25.1 9.5 %collective-permute-start.12 = (bf16[528,128]{1,0:T(8,128)(2,1)S(1)}, bf16[528,128]{1,0:T(8,128)(2,1)S(1)}, u32[]{:S(2)}, u32[]{:S(2)}) collective-permute-start(bf16[528,128]{1,0:T(8,128)(2,1)S(1)} %get-tuple-element.192), channel_id=1, source_target_pairs={{0,1},{1,0},{2,3},{3,2},{4,5},{5,4},{6,7},{7,6},{8,9},{9,8},{10,11... | collective-permute-start | bytes 405512 | tf_op jit(solution)/shard_map/ppermute | solution.py:463
  26.0 7.2 %collective-permute-start.16 = (bf16[528,128]{1,0:T(8,128)(2,1)S(1)}, bf16[528,128]{1,0:T(8,128)(2,1)S(1)}, u32[]{:S(2)}, u32[]{:S(2)}) collective-permute-start(bf16[528,128]{1,0:T(8,128)(2,1)S(1)} %get-tuple-element.184.refs_4_), channel_id=1, source_target_pairs={{0,1},{1,0},{2,3},{3,2},{4,5},{5,4},{6,7},{7,6},{8,9},{9,8},{10,11... | collective-permute-start | bytes 405512 | tf_op jit(solution)/shard_map/ppermute | solution.py:463
  30.0 6.0 %collective-permute-start.13 = (bf16[448,128]{1,0:T(8,128)(2,1)S(1)}, bf16[448,128]{1,0:T(8,128)(2,1)S(1)}, u32[]{:S(2)}, u32[]{:S(2)}) collective-permute-start(bf16[448,128]{1,0:T(8,128)(2,1)S(1)} %get-tuple-element.195), channel_id=1, source_target_pairs={{0,1},{1,0},{2,3},{3,2},{4,5},{5,4},{6,7},{7,6},{8,9},{9,8},{10,11... | collective-permute-start | bytes 344072 | tf_op jit(solution)/shard_map/ppermute | solution.py:463
  33.2 10.3 %collective-permute-start.17 = (bf16[528,128]{1,0:T(8,128)(2,1)S(1)}, bf16[528,128]{1,0:T(8,128)(2,1)S(1)}, u32[]{:S(2)}, u32[]{:S(2)}) collective-permute-start(bf16[528,128]{1,0:T(8,128)(2,1)S(1)} %merge.3), channel_id=1, source_target_pairs={{0,2},{1,3},{2,0},{3,1},{4,6},{5,7},{6,4},{7,5},{8,10},{9,11},{10,... | collective-permute-start | bytes 405512 | tf_op jit(solution)/shard_map/ppermute | solution.py:463
  34.6 4.3 %copy-start.2 = (bf16[704,360]{1,0:T(8,128)(2,1)S(1)}, bf16[704,360]{1,0:T(8,128)(2,1)}, u32[]{:S(2)}) copy-start(bf16[704,360]{1,0:T(8,128)(2,1)} %get-tuple-element.186.refs_2_) | copy-start | bytes 1520644
  34.6 4.3 %copy-start.3 = (bf16[576,360]{1,0:T(8,128)(2,1)S(1)}, bf16[576,360]{1,0:T(8,128)(2,1)}, u32[]{:S(2)}) copy-start(bf16[576,360]{1,0:T(8,128)(2,1)} %get-tuple-element.180.refs_0_) | copy-start | bytes 1244164
  36.0 8.7 %collective-permute-start.14 = (bf16[448,128]{1,0:T(8,128)(2,1)S(1)}, bf16[448,128]{1,0:T(8,128)(2,1)S(1)}, u32[]{:S(2)}, u32[]{:S(2)}) collective-permute-start(bf16[448,128]{1,0:T(8,128)(2,1)S(1)} %get-tuple-element.197), channel_id=1, source_target_pairs={{0,2},{1,3},{2,0},{3,1},{4,6},{5,7},{6,4},{7,5},{8,10},{9,11},{10,... | collective-permute-start | bytes 344072 | tf_op jit(solution)/shard_map/ppermute | solution.py:463
  37.0 7.7 %collective-permute-start.15 = (bf16[448,128]{1,0:T(8,128)(2,1)S(1)}, bf16[448,128]{1,0:T(8,128)(2,1)}, u32[]{:S(2)}, u32[]{:S(2)}) collective-permute-start(bf16[448,128]{1,0:T(8,128)(2,1)S(1)} %get-tuple-element.198), channel_id=1, source_target_pairs={{0,1},{1,0},{2,3},{3,2},{4,5},{5,4},{6,7},{7,6},{8,9},{9,8},{10,11... | collective-permute-start | bytes 344072 | tf_op jit(solution)/shard_map/ppermute | solution.py:463
  43.5 1.2 %copy-start.5 = (f32[170,320]{1,0:T(8,128)S(1)}, f32[170,320]{1,0:T(8,128)}, u32[]{:S(2)}) copy-start(f32[170,320]{1,0:T(8,128)} %get-tuple-element.183.token_ref) | copy-start | bytes 652804
  43.5 1.2 %copy-start.6 = (f32[170,320]{1,0:T(8,128)S(1)}, f32[170,320]{1,0:T(8,128)}, u32[]{:S(2)}) copy-start(f32[170,320]{1,0:T(8,128)} %get-tuple-element.199) | copy-start | bytes 652804
  43.5 1.2 %copy-start.7 = (f32[170,320]{1,0:T(8,128)S(1)}, f32[170,320]{1,0:T(8,128)}, u32[]{:S(2)}) copy-start(f32[170,320]{1,0:T(8,128)} %get-tuple-element.200) | copy-start | bytes 652804
  44.8 5.9 %collective-permute-start.4 = (bf16[528,128]{1,0:T(8,128)(2,1)S(1)}, bf16[528,128]{1,0:T(8,128)(2,1)S(1)}, u32[]{:S(2)}, u32[]{:S(2)}) collective-permute-start(bf16[528,128]{1,0:T(8,128)(2,1)S(1)} %get-tuple-element.125), channel_id=1, source_target_pairs={{0,16},{4,20},{8,24},{12,28},{16,0},{20,4},{24,8},{28,12},{1,17},{... | collective-permute-start | bytes 405512 | tf_op jit(solution)/shard_map/cond/branch_2_fun/ppermute | solution.py:459
  47.6 4.9 %collective-permute-start.5 = (bf16[448,128]{1,0:T(8,128)(2,1)S(1)}, bf16[448,128]{1,0:T(8,128)(2,1)S(1)}, u32[]{:S(2)}, u32[]{:S(2)}) collective-permute-start(bf16[448,128]{1,0:T(8,128)(2,1)S(1)} %get-tuple-element.129), channel_id=1, source_target_pairs={{0,16},{4,20},{8,24},{12,28},{16,0},{20,4},{24,8},{28,12},{1,17},{... | collective-permute-start | bytes 344072 | tf_op jit(solution)/shard_map/cond/branch_2_fun/ppermute | solution.py:459

commit v2 on v1

--- a/solution.py
+++ b/solution.py
@@ -1,4 +1,5 @@
 import functools
+import math
 
 import jax
 import jax.numpy as jnp
@@ -178,11 +179,6 @@
 
 def sigmoid(values):
     return 0.5 * jnp.tanh(0.5 * values) + 0.5
-
-
-def silu_grad(values):
-    gate = sigmoid(values)
-    return gate * (1.0 + values * (1.0 - gate))
 
 
 def cast_kernel(pack, push_ref, params_ref, token_ref, other_token_ref, out_ref, rows_ref):
@@ -265,11 +261,22 @@
     shift = shift_ref[...]
     sums = position_sums([hidden_ref[i * positions : (i + 1) * positions, :] for i in range(samples)])
     offset = shift - table_mean(sums + positions * shift)
-    squares = squares_sums(samples, positions, ROW_STEP, load, offset)
+    squares = squares_sums(samples, positions, math.gcd(positions, ROW_STEP), load, offset)
     inverse = lax.rsqrt(table_mean(squares) + NORM_EPS)
     scales = 0.5 * inverse
     norm_back(
-        table_mean, samples, positions, ROW_STEP, load, scales, offset * scales, inverse, incoming, doubled_ref, store, lambda i: None
+        table_mean,
+        samples,
+        positions,
+        math.gcd(positions, ROW_STEP),
+        load,
+        scales,
+        offset * scales,
+        inverse,
+        incoming,
+        doubled_ref,
+        store,
+        lambda i: None,
     )
     copy = pltpu.make_async_copy(kept_ref, grad_hidden_ref, sems.at[1])
     copy.start()
@@ -316,8 +323,8 @@
             slot = jnp.bitwise_xor(me_ref[0], block)
             rows_ref[block * rows : (block + 1) * rows, : pack.columns] = weight_ref[
                 pl.ds(pl.multiple_of(slot * pack.deep, TILE_ROWS), pack.deep), :
-            ][:rows]
-        weights.append(rows_ref[:, : pack.columns])
+            ].astype(jnp.float32)[:rows]
+        weights.append(rows_ref[:, : pack.columns].astype(jnp.bfloat16))
     grad_act = 0.0
     for index, (grad_ref, weight) in enumerate(zip(grad_refs, weights)):
         grad_act += lax.dot_general(
@@ -346,7 +353,7 @@
 
     scales = 0.5 * inverse
     norm_back(
-        table_mean, samples, positions, ROW_STEP // 2, load, scales, -mean_ref[...] * scales, inverse, incoming, act_ref, store, stored
+        table_mean, samples, positions, math.gcd(positions, ROW_STEP // 2), load, scales, -mean_ref[...] * scales, inverse, incoming, act_ref, store, stored
     )
     for copy in carried_copies + copies[-samples:]:
         copy.wait()
@@ -652,7 +659,7 @@
             [SCALARS] + [BLOCKS] * 3 + [IN_HBM] + [BLOCKS] * (2 * len(packs)) + [IN_HBM] * len(carried),
             operands[:4] + (stay(operands[4]),) + operands[5:] + tuple(map(stay, carried)),
             scratch=[
-                pltpu.VMEM((channels, max(pack.columns for pack in packs)), jnp.bfloat16),
+                pltpu.VMEM((channels, max(pack.columns for pack in packs)), jnp.float32),
                 pltpu.VMEM(block_input.shape, jnp.bfloat16),
                 pltpu.VMEM(block_input.shape, jnp.bfloat16),
                 pltpu.VMEM((tokens, channels), jnp.float32),

time: 53.8 us -> 53.7 us (level); the launches traced: 53.5 us -> 54.3 us
  starting transfers between devices: 17.7 us -> 18.7 us
    ppermute x2, starting transfers between devices: 2.16 us -> 3.09 us  [moved_on(): lax.ppermute(block, axis, [(i, (i + distance) % size) for i in range(size)])]
  transfers between devices with their start and end apart: 14 -> 14, of which waited for: 7 -> 8; matrix products, arithmetic and copies ran while one was open for 0% -> 0% of each run, Pallas kernels for 42% -> 41%
where the time goes in v2:
time: 53.7 us; the launch traced here: 54.3 us
  Pallas kernels  23.5 us (44%)
  starting transfers between devices  18.7 us (35%)
  waiting for transfers between devices  8.23 us (15%)
  between operations  2.22 us (4%)
  local copies, waits for them, and re-layouts  1.62 us (3%)
    pallas_call x16, Pallas kernels, call(): pl.pallas_call(kernel, out_shape=outs, in_specs=specs, out_specs=out_spec...  23.5 us
    ppermute x12, starting transfers between devices, exchanged(): lax.ppermute(block, axis, [(i, i ^ bit) for i in range(lax.axis_size(axis...  15.6 us
    ppermute x12, waiting for transfers between devices, exchanged(): lax.ppermute(block, axis, [(i, i ^ bit) for i in range(lax.axis_size(axis...  7.55 us
    ppermute x2, starting transfers between devices, moved_on(): lax.ppermute(block, axis, [(i, (i + distance) % size) for i in range(size)])  3.09 us
    unnamed x16, local copies, waits for them, and re-layouts  1.62 us
  transfers between devices with their start and end apart: 14, of which 8 were waited for; matrix products, arithmetic and copies ran while one was open for 0% of the time, Pallas kernels for 41%

profile of v2, /device:TPU:0, one launch (start us, length us, event | category | flops | bytes accessed | tf_op | source)
XLA Modules:
  0.0 54.3 jit_solution(2130669355258762559)
XLA Ops:
  1.3 0.0 copy-start
  1.3 1.0 %copy-done = f32[1,170,680]{2,0,1:T(1,128)S(1)} copy-done((f32[1,170,680]{2,0,1:T(1,128)S(1)}, f32[1,170,680]{2,0,1:T(1,128)}, u32[]{:S(2)}) %copy-start) | copy-done | bytes 462424
  2.3 0.2 cast.2.refs_0_
  2.5 3.1 %collective-permute-start.6 = (bf16[528,128]{1,0:T(8,128)(2,1)S(1)}, bf16[528,128]{1,0:T(8,128)(2,1)S(1)}, u32[]{:S(2)}, u32[]{:S(2)}) collective-permute-start(bf16[528,128]{1,0:T(8,128)(2,1)S(1)} %cast.2.refs_0_), channel_id=1, source_target_pairs={{0,1},{1,0},{2,3},{3,2},{4,5},{5,4},{6,7},{7,6},{8,9},{9,8},{10,11... | collective-permute-start | bytes 405512 | tf_op jit(solution)/shard_map/ppermute | solution.py:470
  5.6 2.6 %collective-permute-start.7 = (bf16[528,128]{1,0:T(8,128)(2,1)S(1)}, bf16[528,128]{1,0:T(8,128)(2,1)S(1)}, u32[]{:S(2)}, u32[]{:S(2)}) collective-permute-start(bf16[528,128]{1,0:T(8,128)(2,1)S(1)} %cast.2.refs_0_), channel_id=1, source_target_pairs={{0,2},{1,3},{2,0},{3,1},{4,6},{5,7},{6,4},{7,5},{8,10},{9,11},{10,... | collective-permute-start | bytes 405512 | tf_op jit(solution)/shard_map/ppermute | solution.py:470
  9.0 0.0 copy-start.4
  9.0 0.1 pad_maximum_fusion.scales_ref
  9.1 0.6 %copy-done.4 = bf16[2,680]{1,0:T(2,128)(2,1)S(1)} copy-done((bf16[2,680]{1,0:T(2,128)(2,1)S(1)}, bf16[2,680]{1,0:T(2,128)(2,1)}, u32[]{:S(2)}) %copy-start.4) | copy-done | bytes 2744
  9.7 3.4 %norm_in.1 = (bf16[704,576]{1,0:T(8,128)(2,1)S(1)}, f32[2,680]{1,0:T(2,128)S(1)}, f32[2,680]{1,0:T(2,128)S(1)}, bf16[360,360]{1,0:T(8,128)(2,1)S(1)}, f32[2,360]...) custom-call(s32[1]{0:T(128)} %bitcast.3.me_ref, ...), custom_call_target="tpu_custom_call" | custom-call | bytes 3133440 | tf_op jit(solution)/shard_map/norm_in/pallas_call | solution.py:448
  13.0 0.0 collective-permute-done.6.refs_1_.token_ref
  13.0 0.0 copy-done.1
  13.0 0.3 cast.3.refs_0_
  13.3 0.4 collective-permute-start.10
  13.7 0.8 %collective-permute-done.7.refs_2_ = bf16[528,128]{1,0:T(8,128)(2,1)S(1)} collective-permute-done((bf16[528,128]{1,0:T(8,128)(2,1)S(1)}, bf16[528,128]{1,0:T(8,128)(2,1)S(1)}, u32[]{:S(2)}, u32[]{:S(2)}) %collective-permute-start.7) | collective-permute-done | bytes 135200 | tf_op jit(solution)/shard_map/ppermute | solution.py:470
  14.5 1.0 %collective-permute-start.8 = (bf16[528,128]{1,0:T(8,128)(2,1)S(1)}, bf16[528,128]{1,0:T(8,128)(2,1)S(1)}, u32[]{:S(2)}, u32[]{:S(2)}) collective-permute-start(bf16[528,128]{1,0:T(8,128)(2,1)S(1)} %collective-permute-done.7.refs_2_), channel_id=1, source_target_pairs={{0,1},{1,0},{2,3},{3,2},{4,5},{5,4},{6,7},{7,6},{8,9},{9,8},{10,11... | collective-permute-start | bytes 405512 | tf_op jit(solution)/shard_map/ppermute | solution.py:470
  15.5 2.4 %cut.1 = (f32[170,360]{1,0:T(8,128)}, f32[170,360]{1,0:T(8,128)}, f32[170,360]{1,0:T(8,128)}, f32[170,320]{1,0:T(8,128)}, f32[170,320]{1,0:T(8,128)}, /*index=5*/f32[170,320]{1,0:T(8,128)}) custom-call(f32[170,1,680]{2,1,0:T(1,128)} %bitcast.13, f32[170,1,680]{2,1,0:T(1,128)} %bitcast.18, f32[170,1,680]{2,1,0:T(1,128)} %bitcast.22, ...), custom_call_target="tpu_custom_call" | custom-call | bytes 924800 | tf_op jit(solution)/shard_map/cut/pallas_call | solution.py:448
  17.9 1.0 %collective-permute-start.9 = (bf16[448,128]{1,0:T(8,128)(2,1)S(1)}, bf16[448,128]{1,0:T(8,128)(2,1)S(1)}, u32[]{:S(2)}, u32[]{:S(2)}) collective-permute-start(bf16[448,128]{1,0:T(8,128)(2,1)S(1)} %cast.3.refs_0_), channel_id=1, source_target_pairs={{0,1},{1,0},{2,3},{3,2},{4,5},{5,4},{6,7},{7,6},{8,9},{9,8},{10,11... | collective-permute-start | bytes 344072 | tf_op jit(solution)/shard_map/ppermute | solution.py:470
  19.0 2.1 %collective-permute-done.10.block_ref = bf16[448,128]{1,0:T(8,128)(2,1)S(1)} collective-permute-done((bf16[448,128]{1,0:T(8,128)(2,1)S(1)}, bf16[448,128]{1,0:T(8,128)(2,1)S(1)}, u32[]{:S(2)}, u32[]{:S(2)}) %collective-permute-start.10) | collective-permute-done | bytes 114720 | tf_op jit(solution)/shard_map/ppermute | solution.py:470
  21.1 0.1 collective-permute-start.11
  21.2 1.2 %collective-permute-done.8.refs_3_ = bf16[528,128]{1,0:T(8,128)(2,1)S(1)} collective-permute-done((bf16[528,128]{1,0:T(8,128)(2,1)S(1)}, bf16[528,128]{1,0:T(8,128)(2,1)S(1)}, u32[]{:S(2)}, u32[]{:S(2)}) %collective-permute-start.8) | collective-permute-done | bytes 135200 | tf_op jit(solution)/shard_map/ppermute | solution.py:470
  22.3 2.8 %mix.2 = (bf16[576,360]{1,0:T(8,128)(2,1)}, bf16[704,360]{1,0:T(8,128)(2,1)}, f32[176,360]{1,0:T(8,128)S(1)}, bf16[528,128]{1,0:T(8,128)(2,1)S(1)}, bf16[528,128...) custom-call(bf16[704,576]{1,0:T(8,128)(2,1)S(1)} %get-tuple-element.177.act_ref, ...), custom_call_target="tpu_custom_call" | custom-call | flops 564019200 | bytes 1658880 | tf_op jit(solution)/shard_map/mix/pallas_call | solution.py:448
  25.1 0.9 %collective-permute-start.12 = (bf16[528,128]{1,0:T(8,128)(2,1)S(1)}, bf16[528,128]{1,0:T(8,128)(2,1)S(1)}, u32[]{:S(2)}, u32[]{:S(2)}) collective-permute-start(bf16[528,128]{1,0:T(8,128)(2,1)S(1)} %get-tuple-element.192), channel_id=1, source_target_pairs={{0,1},{1,0},{2,3},{3,2},{4,5},{5,4},{6,7},{7,6},{8,9},{9,8},{10,11... | collective-permute-start | bytes 405512 | tf_op jit(solution)/shard_map/ppermute | solution.py:470
  26.0 1.2 %collective-permute-start.16 = (bf16[528,128]{1,0:T(8,128)(2,1)S(1)}, bf16[528,128]{1,0:T(8,128)(2,1)S(1)}, u32[]{:S(2)}, u32[]{:S(2)}) collective-permute-start(bf16[528,128]{1,0:T(8,128)(2,1)S(1)} %get-tuple-element.184.refs_4_), channel_id=1, source_target_pairs={{0,1},{1,0},{2,3},{3,2},{4,5},{5,4},{6,7},{7,6},{8,9},{9,8},{10,11... | collective-permute-start | bytes 405512 | tf_op jit(solution)/shard_map/ppermute | solution.py:470
  27.2 0.0 collective-permute-done.9.refs_1_
  27.2 0.0 collective-permute-done.11.refs_3_
  27.2 2.8 %mix.3 = (bf16[576,320]{1,0:T(8,128)(2,1)S(1)}, bf16[704,320]{1,0:T(8,128)(2,1)S(1)}, bf16[448,128]{1,0:T(8,128)(2,1)S(1)}) custom-call(bf16[704,576]{1,0:T(8,128)(2,1)S(1)} %get-tuple-element.177.act_ref, f32[2,320]{1,0:T(2,128)S(1)} %get-tuple-element.181.shift_ref, bf16[2,288,320]{2,1,0:T(8,128)(2,1)S(1)} %get-tuple-element.182.out_grad_ref, ...), custom_call_target="tpu_custom_call" | custom-call | flops 501350400 | bytes 1474560 | tf_op jit(solution)/shard_map/mix/pallas_call | solution.py:448
  30.0 0.9 %collective-permute-start.13 = (bf16[448,128]{1,0:T(8,128)(2,1)S(1)}, bf16[448,128]{1,0:T(8,128)(2,1)S(1)}, u32[]{:S(2)}, u32[]{:S(2)}) collective-permute-start(bf16[448,128]{1,0:T(8,128)(2,1)S(1)} %get-tuple-element.195), channel_id=1, source_target_pairs={{0,1},{1,0},{2,3},{3,2},{4,5},{5,4},{6,7},{7,6},{8,9},{9,8},{10,11... | collective-permute-start | bytes 344072 | tf_op jit(solution)/shard_map/ppermute | solution.py:470
  30.9 2.3 %collective-permute-done.16.other_ref = bf16[528,128]{1,0:T(8,128)(2,1)S(1)} collective-permute-done((bf16[528,128]{1,0:T(8,128)(2,1)S(1)}, bf16[528,128]{1,0:T(8,128)(2,1)S(1)}, u32[]{:S(2)}, u32[]{:S(2)}) %collective-permute-start.16) | collective-permute-done | bytes 135200 | tf_op jit(solution)/shard_map/ppermute | solution.py:470
  33.2 1.4 %collective-permute-start.17 = (bf16[528,128]{1,0:T(8,128)(2,1)S(1)}, bf16[528,128]{1,0:T(8,128)(2,1)S(1)}, u32[]{:S(2)}, u32[]{:S(2)}) collective-permute-start(bf16[528,128]{1,0:T(8,128)(2,1)S(1)} %merge.3), channel_id=1, source_target_pairs={{0,2},{1,3},{2,0},{3,1},{4,6},{5,7},{6,4},{7,5},{8,10},{9,11},{10,... | collective-permute-start | bytes 405512 | tf_op jit(solution)/shard_map/ppermute | solution.py:470
  34.6 0.0 collective-permute-done.12.token_ref.refs_0_
  34.6 0.7 %rest.1 = (f32[176,320]{1,0:T(8,128)S(1)}, bf16[448,128]{1,0:T(8,128)(2,1)S(1)}, bf16[448,128]{1,0:T(8,128)(2,1)S(1)}) custom-call(bf16[704,576]{1,0:T(8,128)(2,1)S(1)} %get-tuple-element.177.act_ref, bf16[576,320]{1,0:T(8,128)(2,1)S(1)} %get-tuple-element.185.refs_1_.grad_hidden_ref, bf16[528,128]{1,0:T(8,128)(2,1)S(1)} %collective-permute-done.12.token_ref.refs_0_), custom_call_target="tpu_custom_call" | custom-call | flops 250675200 | tf_op jit(solution)/shard_map/rest/pallas_call | solution.py:448
  35.3 0.7 %collective-permute-done.13.other_ref = bf16[448,128]{1,0:T(8,128)(2,1)S(1)} collective-permute-done((bf16[448,128]{1,0:T(8,128)(2,1)S(1)}, bf16[448,128]{1,0:T(8,128)(2,1)S(1)}, u32[]{:S(2)}, u32[]{:S(2)}) %collective-permute-start.13) | collective-permute-done | bytes 114720 | tf_op jit(solution)/shard_map/ppermute | solution.py:470
  36.0 1.0 %collective-permute-start.14 = (bf16[448,128]{1,0:T(8,128)(2,1)S(1)}, bf16[448,128]{1,0:T(8,128)(2,1)S(1)}, u32[]{:S(2)}, u32[]{:S(2)}) collective-permute-start(bf16[448,128]{1,0:T(8,128)(2,1)S(1)} %get-tuple-element.197), channel_id=1, source_target_pairs={{0,2},{1,3},{2,0},{3,1},{4,6},{5,7},{6,4},{7,5},{8,10},{9,11},{10,... | collective-permute-start | bytes 344072 | tf_op jit(solution)/shard_map/ppermute | solution.py:470
  37.0 2.0 %collective-permute-start.15 = (bf16[448,128]{1,0:T(8,128)(2,1)S(1)}, bf16[448,128]{1,0:T(8,128)(2,1)}, u32[]{:S(2)}, u32[]{:S(2)}) collective-permute-start(bf16[448,128]{1,0:T(8,128)(2,1)S(1)} %get-tuple-element.198), channel_id=1, source_target_pairs={{0,1},{1,0},{2,3},{3,2},{4,5},{5,4},{6,7},{7,6},{8,9},{9,8},{10,11... | collective-permute-start | bytes 344072 | tf_op jit(solution)/shard_map/ppermute | solution.py:470
  39.0 4.3 %input_grad.1 = (bf16[2,288,680]{2,1,0:T(8,128)(2,1)}, f32[170,360]{1,0:T(8,128)S(1)}, f32[170,360]{1,0:T(8,128)S(1)}, f32[170,360]{1,0:T(8,128)S(1)}) custom-call(s32[1]{0:T(128)} %bitcast.3.me_ref, f32[2,680]{1,0:T(2,128)S(1)} %get-tuple-element.174.refs_4_.other_token_ref.refs_3_.mean_ref, f32[2,680]{1,0:T(2,128)S(1)} %get-tuple-element.175.inverse_ref, ...), custom_call_target="tpu_custom_call" | custom-call | flops 532684800 | bytes 3133440 | tf_op jit(solution)/shard_map/input_grad/pallas_call | solution.py:448
  43.3 0.2 collective-permute-done.17.refs_1_
  43.5 0.9 %adam.7 = (f32[176,360]{1,0:T(8,128)S(1)}, f32[176,360]{1,0:T(8,128)S(1)}, bf16[528,128]{1,0:T(8,128)(2,1)S(1)}) custom-call(f32[4]{0:T(128)S(1)} %pad_maximum_fusion.scales_ref, f32[176,360]{1,0:T(8,128)S(1)} %get-tuple-element.201.own_ref, bf16[528,128]{1,0:T(8,128)(2,1)S(1)} %collective-permute-done.12.token_ref.refs_0_, ...), custom_call_target="tpu_custom_call" | custom-call | bytes 489600 | tf_op jit(solution)/shard_map/adam/pallas_call | solution.py:448
  44.4 0.3 collective-permute-done.14
  44.7 0.0 collective-permute-done.15
  44.7 9.6 %conditional.1 = (f32[170,1,680]{2,1,0:T(1,128)}, f32[170,1,680]{2,1,0:T(1,128)}, f32[1]{0:T(128)}, f32[1,170,680]{2,0,1:T(1,128)}) conditional(s32[]{:T(128)} %clamp.3, (f32[4]{0:T(128)S(1)}, f32[176,320]{1,0:T(8,128)S(1)}, bf16[448,128]{1,0:T(8,128)(2,1)S(1)}, bf16[448,128]{1,0:T(8,128)(2,1)}, f32[170,320]{1,0:T(8,128)S(1)}, ...), branch_computations={%region_0.1_spmd, %region_1.2_spmd, %region_2.3_spmd} | conditional | bytes 3773936 | solution.py:689
  44.8 1.5 %collective-permute-start.2 = (bf16[528,128]{1,0:T(8,128)(2,1)S(1)}, bf16[528,128]{1,0:T(8,128)(2,1)S(1)}, u32[]{:S(2)}, u32[]{:S(2)}) collective-permute-start(bf16[528,128]{1,0:T(8,128)(2,1)S(1)} %get-tuple-element.106), channel_id=1, source_target_pairs={{0,8},{4,12},{8,16},{12,20},{16,24},{20,28},{24,0},{28,4},{1,9},{5... | collective-permute-start | bytes 405512 | tf_op jit(solution)/shard_map/cond/branch_1_fun/ppermute | solution.py:466
  46.3 1.3 %adam.5 = (f32[176,320]{1,0:T(8,128)S(1)}, f32[176,320]{1,0:T(8,128)S(1)}, bf16[448,128]{1,0:T(8,128)(2,1)S(1)}) custom-call(f32[4]{0:T(128)S(1)} %get-tuple-element.95.scales_ref, f32[176,320]{1,0:T(8,128)S(1)} %get-tuple-element.96.own_ref, bf16[448,128]{1,0:T(8,128)(2,1)S(1)} %get-tuple-element.97.refs_0_, bf16[448,128]{1,0:T(8,128)(2,1)} %get-tuple-element.98.refs_1_, ...), custom_call_target="tpu_custom_call" | custom-call | bytes 435200 | tf_op jit(solution)/shard_map/cond/branch_1_fun/adam/pallas_call | solution.py:448
  47.6 1.5 %collective-permute-start.3 = (bf16[448,128]{1,0:T(8,128)(2,1)S(1)}, bf16[448,128]{1,0:T(8,128)(2,1)S(1)}, u32[]{:S(2)}, u32[]{:S(2)}) collective-permute-start(bf16[448,128]{1,0:T(8,128)(2,1)S(1)} %get-tuple-element.110), channel_id=1, source_target_pairs={{0,8},{4,12},{8,16},{12,20},{16,24},{20,28},{24,0},{28,4},{1,9},{5... | collective-permute-start | bytes 344072 | tf_op jit(solution)/shard_map/cond/branch_1_fun/ppermute | solution.py:466
  49.1 2.4 %moments.4 = (f32[170,1,680]{2,1,0:T(1,128)}, f32[170,1,680]{2,1,0:T(1,128)}) custom-call(f32[170,1,680]{2,1,0:T(1,128)} %get-tuple-element.92.first_hbm, f32[170,1,680]{2,1,0:T(1,128)} %get-tuple-element.93.second_hbm, f32[176,360]{1,0:T(8,128)S(1)} %get-tuple-element.94.refs_0_, f32[176,320]{1,0:T(8,128)S(1)} %get-tuple-element.102.refs_1_), custom_call_target="tpu_custom_call" | custom-call | bytes 924800 | tf_op jit(solution)/shard_map/cond/branch_1_fun/moments/pallas_call | solution.py:448
  51.6 0.0 collective-permute-done.2.other_ref
  51.6 1.1 %half_average.4 = (f32[176,360]{1,0:T(8,128)S(1)}, f32[1]{0:T(128)}) custom-call(f32[4]{0:T(128)S(1)} %get-tuple-element.95.scales_ref, f32[176,360]{1,0:T(8,128)S(1)} %get-tuple-element.105.moved_ref, bf16[528,128]{1,0:T(8,128)(2,1)S(1)} %collective-permute-done.2.other_ref), custom_call_target="tpu_custom_call" | custom-call | bytes 489600 | tf_op jit(solution)/shard_map/cond/branch_1_fun/half_average/pallas_call | solution.py:448
  52.6 0.7 %collective-permute-done.3.other_ref = bf16[448,128]{1,0:T(8,128)(2,1)S(1)} collective-permute-done((bf16[448,128]{1,0:T(8,128)(2,1)S(1)}, bf16[448,128]{1,0:T(8,128)(2,1)S(1)}, u32[]{:S(2)}, u32[]{:S(2)}) %collective-permute-start.3) | collective-permute-done | bytes 114720 | tf_op jit(solution)/shard_map/cond/branch_1_fun/ppermute | solution.py:466
  53.3 1.0 %average.4 = f32[170,1,680]{2,1,0:T(1,128)} custom-call(f32[176,360]{1,0:T(8,128)S(1)} %get-tuple-element.108.mean_ref, f32[176,320]{1,0:T(8,128)S(1)} %get-tuple-element.109.moved_ref, bf16[448,128]{1,0:T(8,128)(2,1)S(1)} %collective-permute-done.3.other_ref), custom_call_target="tpu_custom_call" | custom-call | bytes 924800 | tf_op jit(solution)/shard_map/cond/branch_1_fun/average/pallas_call | solution.py:448
  (14 shorter events, 0.1 us)
Async XLA Ops:
  1.3 1.0 %copy-start = (f32[1,170,680]{2,0,1:T(1,128)S(1)}, f32[1,170,680]{2,0,1:T(1,128)}, u32[]{:S(2)}) copy-start(f32[1,170,680]{2,0,1:T(1,128)} %param.14) | copy-start | bytes 1387204
  2.5 10.5 %collective-permute-start.6 = (bf16[528,128]{1,0:T(8,128)(2,1)S(1)}, bf16[528,128]{1,0:T(8,128)(2,1)S(1)}, u32[]{:S(2)}, u32[]{:S(2)}) collective-permute-start(bf16[528,128]{1,0:T(8,128)(2,1)S(1)} %cast.2.refs_0_), channel_id=1, source_target_pairs={{0,1},{1,0},{2,3},{3,2},{4,5},{5,4},{6,7},{7,6},{8,9},{9,8},{10,11... | collective-permute-start | bytes 405512 | tf_op jit(solution)/shard_map/ppermute | solution.py:470
  5.6 8.9 %collective-permute-start.7 = (bf16[528,128]{1,0:T(8,128)(2,1)S(1)}, bf16[528,128]{1,0:T(8,128)(2,1)S(1)}, u32[]{:S(2)}, u32[]{:S(2)}) collective-permute-start(bf16[528,128]{1,0:T(8,128)(2,1)S(1)} %cast.2.refs_0_), channel_id=1, source_target_pairs={{0,2},{1,3},{2,0},{3,1},{4,6},{5,7},{6,4},{7,5},{8,10},{9,11},{10,... | collective-permute-start | bytes 405512 | tf_op jit(solution)/shard_map/ppermute | solution.py:470
  9.0 0.7 %copy-start.4 = (bf16[2,680]{1,0:T(2,128)(2,1)S(1)}, bf16[2,680]{1,0:T(2,128)(2,1)}, u32[]{:S(2)}) copy-start(bf16[2,680]{1,0:T(2,128)(2,1)} %shift_ref.1) | copy-start | bytes 8164
  9.7 3.4 %copy-start.1 = (f32[1,170,680]{2,0,1:T(1,128)S(1)}, f32[1,170,680]{2,0,1:T(1,128)}, u32[]{:S(2)}) copy-start(f32[1,170,680]{2,0,1:T(1,128)} %param.14) | copy-start | bytes 1387204
  13.3 7.7 %collective-permute-start.10 = (bf16[448,128]{1,0:T(8,128)(2,1)S(1)}, bf16[448,128]{1,0:T(8,128)(2,1)S(1)}, u32[]{:S(2)}, u32[]{:S(2)}) collective-permute-start(bf16[448,128]{1,0:T(8,128)(2,1)S(1)} %cast.3.refs_0_), channel_id=1, source_target_pairs={{0,2},{1,3},{2,0},{3,1},{4,6},{5,7},{6,4},{7,5},{8,10},{9,11},{10,... | collective-permute-start | bytes 344072 | tf_op jit(solution)/shard_map/ppermute | solution.py:470
  14.5 7.9 %collective-permute-start.8 = (bf16[528,128]{1,0:T(8,128)(2,1)S(1)}, bf16[528,128]{1,0:T(8,128)(2,1)S(1)}, u32[]{:S(2)}, u32[]{:S(2)}) collective-permute-start(bf16[528,128]{1,0:T(8,128)(2,1)S(1)} %collective-permute-done.7.refs_2_), channel_id=1, source_target_pairs={{0,1},{1,0},{2,3},{3,2},{4,5},{5,4},{6,7},{7,6},{8,9},{9,8},{10,11... | collective-permute-start | bytes 405512 | tf_op jit(solution)/shard_map/ppermute | solution.py:470
  17.9 9.3 %collective-permute-start.9 = (bf16[448,128]{1,0:T(8,128)(2,1)S(1)}, bf16[448,128]{1,0:T(8,128)(2,1)S(1)}, u32[]{:S(2)}, u32[]{:S(2)}) collective-permute-start(bf16[448,128]{1,0:T(8,128)(2,1)S(1)} %cast.3.refs_0_), channel_id=1, source_target_pairs={{0,1},{1,0},{2,3},{3,2},{4,5},{5,4},{6,7},{7,6},{8,9},{9,8},{10,11... | collective-permute-start | bytes 344072 | tf_op jit(solution)/shard_map/ppermute | solution.py:470
  21.1 6.1 %collective-permute-start.11 = (bf16[448,128]{1,0:T(8,128)(2,1)S(1)}, bf16[448,128]{1,0:T(8,128)(2,1)S(1)}, u32[]{:S(2)}, u32[]{:S(2)}) collective-permute-start(bf16[448,128]{1,0:T(8,128)(2,1)S(1)} %hold.1.refs_2_), channel_id=1, source_target_pairs={{0,1},{1,0},{2,3},{3,2},{4,5},{5,4},{6,7},{7,6},{8,9},{9,8},{10,11... | collective-permute-start | bytes 344072 | tf_op jit(solution)/shard_map/ppermute | solution.py:470
  25.1 9.5 %collective-permute-start.12 = (bf16[528,128]{1,0:T(8,128)(2,1)S(1)}, bf16[528,128]{1,0:T(8,128)(2,1)S(1)}, u32[]{:S(2)}, u32[]{:S(2)}) collective-permute-start(bf16[528,128]{1,0:T(8,128)(2,1)S(1)} %get-tuple-element.192), channel_id=1, source_target_pairs={{0,1},{1,0},{2,3},{3,2},{4,5},{5,4},{6,7},{7,6},{8,9},{9,8},{10,11... | collective-permute-start | bytes 405512 | tf_op jit(solution)/shard_map/ppermute | solution.py:470
  26.0 7.2 %collective-permute-start.16 = (bf16[528,128]{1,0:T(8,128)(2,1)S(1)}, bf16[528,128]{1,0:T(8,128)(2,1)S(1)}, u32[]{:S(2)}, u32[]{:S(2)}) collective-permute-start(bf16[528,128]{1,0:T(8,128)(2,1)S(1)} %get-tuple-element.184.refs_4_), channel_id=1, source_target_pairs={{0,1},{1,0},{2,3},{3,2},{4,5},{5,4},{6,7},{7,6},{8,9},{9,8},{10,11... | collective-permute-start | bytes 405512 | tf_op jit(solution)/shard_map/ppermute | solution.py:470
  30.0 6.0 %collective-permute-start.13 = (bf16[448,128]{1,0:T(8,128)(2,1)S(1)}, bf16[448,128]{1,0:T(8,128)(2,1)S(1)}, u32[]{:S(2)}, u32[]{:S(2)}) collective-permute-start(bf16[448,128]{1,0:T(8,128)(2,1)S(1)} %get-tuple-element.195), channel_id=1, source_target_pairs={{0,1},{1,0},{2,3},{3,2},{4,5},{5,4},{6,7},{7,6},{8,9},{9,8},{10,11... | collective-permute-start | bytes 344072 | tf_op jit(solution)/shard_map/ppermute | solution.py:470
  33.2 10.3 %collective-permute-start.17 = (bf16[528,128]{1,0:T(8,128)(2,1)S(1)}, bf16[528,128]{1,0:T(8,128)(2,1)S(1)}, u32[]{:S(2)}, u32[]{:S(2)}) collective-permute-start(bf16[528,128]{1,0:T(8,128)(2,1)S(1)} %merge.3), channel_id=1, source_target_pairs={{0,2},{1,3},{2,0},{3,1},{4,6},{5,7},{6,4},{7,5},{8,10},{9,11},{10,... | collective-permute-start | bytes 405512 | tf_op jit(solution)/shard_map/ppermute | solution.py:470
  34.6 4.3 %copy-start.2 = (bf16[704,360]{1,0:T(8,128)(2,1)S(1)}, bf16[704,360]{1,0:T(8,128)(2,1)}, u32[]{:S(2)}) copy-start(bf16[704,360]{1,0:T(8,128)(2,1)} %get-tuple-element.186.refs_2_) | copy-start | bytes 1520644
  34.6 4.3 %copy-start.3 = (bf16[576,360]{1,0:T(8,128)(2,1)S(1)}, bf16[576,360]{1,0:T(8,128)(2,1)}, u32[]{:S(2)}) copy-start(bf16[576,360]{1,0:T(8,128)(2,1)} %get-tuple-element.180.refs_0_) | copy-start | bytes 1244164
  36.0 8.7 %collective-permute-start.14 = (bf16[448,128]{1,0:T(8,128)(2,1)S(1)}, bf16[448,128]{1,0:T(8,128)(2,1)S(1)}, u32[]{:S(2)}, u32[]{:S(2)}) collective-permute-start(bf16[448,128]{1,0:T(8,128)(2,1)S(1)} %get-tuple-element.197), channel_id=1, source_target_pairs={{0,2},{1,3},{2,0},{3,1},{4,6},{5,7},{6,4},{7,5},{8,10},{9,11},{10,... | collective-permute-start | bytes 344072 | tf_op jit(solution)/shard_map/ppermute | solution.py:470
  37.0 7.7 %collective-permute-start.15 = (bf16[448,128]{1,0:T(8,128)(2,1)S(1)}, bf16[448,128]{1,0:T(8,128)(2,1)}, u32[]{:S(2)}, u32[]{:S(2)}) collective-permute-start(bf16[448,128]{1,0:T(8,128)(2,1)S(1)} %get-tuple-element.198), channel_id=1, source_target_pairs={{0,1},{1,0},{2,3},{3,2},{4,5},{5,4},{6,7},{7,6},{8,9},{9,8},{10,11... | collective-permute-start | bytes 344072 | tf_op jit(solution)/shard_map/ppermute | solution.py:470
  43.5 1.2 %copy-start.5 = (f32[170,320]{1,0:T(8,128)S(1)}, f32[170,320]{1,0:T(8,128)}, u32[]{:S(2)}) copy-start(f32[170,320]{1,0:T(8,128)} %get-tuple-element.183.token_ref) | copy-start | bytes 652804
  43.5 1.2 %copy-start.6 = (f32[170,320]{1,0:T(8,128)S(1)}, f32[170,320]{1,0:T(8,128)}, u32[]{:S(2)}) copy-start(f32[170,320]{1,0:T(8,128)} %get-tuple-element.199) | copy-start | bytes 652804
  43.5 1.2 %copy-start.7 = (f32[170,320]{1,0:T(8,128)S(1)}, f32[170,320]{1,0:T(8,128)}, u32[]{:S(2)}) copy-start(f32[170,320]{1,0:T(8,128)} %get-tuple-element.200) | copy-start | bytes 652804
  44.8 6.8 %collective-permute-start.2 = (bf16[528,128]{1,0:T(8,128)(2,1)S(1)}, bf16[528,128]{1,0:T(8,128)(2,1)S(1)}, u32[]{:S(2)}, u32[]{:S(2)}) collective-permute-start(bf16[528,128]{1,0:T(8,128)(2,1)S(1)} %get-tuple-element.106), channel_id=1, source_target_pairs={{0,8},{4,12},{8,16},{12,20},{16,24},{20,28},{24,0},{28,4},{1,9},{5... | collective-permute-start | bytes 405512 | tf_op jit(solution)/shard_map/cond/branch_1_fun/ppermute | solution.py:466
  47.6 5.7 %collective-permute-start.3 = (bf16[448,128]{1,0:T(8,128)(2,1)S(1)}, bf16[448,128]{1,0:T(8,128)(2,1)S(1)}, u32[]{:S(2)}, u32[]{:S(2)}) collective-permute-start(bf16[448,128]{1,0:T(8,128)(2,1)S(1)} %get-tuple-element.110), channel_id=1, source_target_pairs={{0,8},{4,12},{8,16},{12,20},{16,24},{20,28},{24,0},{28,4},{1,9},{5... | collective-permute-start | bytes 344072 | tf_op jit(solution)/shard_map/cond/branch_1_fun/ppermute | solution.py:466
